TPU v7x, 32 devices: a whole 2x2x4 slice. The times are simulated.
32 devices in a mesh: group: 4 (over y, x), dom: 8 (over z, core).
Axes of the slice: x: 2, y: 2, z: 4, core: 2. Of those that a mesh axis runs over, the one named last changes fastest.
Arguments:
- mode_shapes: float32 [96, 65536], P(None, ('group', 'dom')), may hold values from -6 to 6
- send_nodes: int32 [32, 1024], P(('group', 'dom')), may hold values from 0 to 2047, as said below
- interp_index: int32 [8, 64, 4096], P(None, 'group', 'dom'), may hold values from -1 to 1023, as said below
- interp_weight: float32 [8, 64, 4096], P(None, 'group', 'dom'), may hold values from 0.1 to 1
- blend: float32 [64, 4096], P('group', 'dom'), may hold values from 0.2 to 1
- motion_gain: float32 [30, 64, 4096], P(None, 'group', 'dom'), may hold values from -3 to 3
- frequency: float32 [32], replicated, may hold values from 0.3 to 3
- volume: float32 [64, 4096], P('group', 'dom'), may hold values from 0.5 to 2
- jacobian: float32 [125, 64, 4096], P(None, 'group', 'dom'), may hold values from -1.2 to 1.2
- state: bfloat16 [320, 64, 4096], P(None, 'group', 'dom'), may hold values from -6 to 6
Outputs:
- mesh_motion: float32 [96, 64, 4096], P(None, 'group', 'dom')
- residual: float32 [320, 64, 4096], P(None, 'group', 'dom')
Inputs may be any that keep to these rules, and one draw needn't show every extreme that they name: `send_nodes`: each entry names a node local to the owner of its row, 0 to 2047. `interp_index`: A live entry is s * 32 + t, naming slot t that owner s sends to the cell's partition; a cell has 1 to 8 live entries, stored first, then -1 for padding; some cell has all 8 live. From each owner a partition uses at most 32 slots.
All inputs are finite; a program needn't handle non-finite values.
Results may differ from a plain program's by a relative error of at most 0.0003.
Values may be sent and summed in bfloat16 or wider, within the bound.
No kernel may reach another device: no remote copies, remote signals or barrier semaphores. Data moves between devices by JAX's collectives and lax.ppermute only.
A program may use at most 192 MiB of HBM per device.

v0:
```python
import jax
import jax.numpy as jnp
from jax import lax
from jax.sharding import PartitionSpec as P

COMP = 3
VARS = 5
CASES = 32


def extended(value, sides, width):
    for axis, dim in sides:
        peers, length = (lax.axis_size(axis), value.shape[dim])
        up = [(i, (i + 1) % peers) for i in range(peers - 1)]
        down = [(j, i) for i, j in up]
        last = lax.slice_in_dim(value, length - width, length, axis=dim)
        initial = lax.slice_in_dim(value, 0, width, axis=dim)
        before = lax.ppermute(last, axis, up)
        after = lax.ppermute(initial, axis, down)
        value = jnp.concatenate([before, value, after], axis=dim)
    return value


def apply_block(block, field):
    total = jnp.zeros(field.shape, jnp.float32)
    for u in range(VARS):
        total = total + block[:, u][None, None] * field[:, :, u][:, :, None].astype(jnp.float32)
    return total


def block_length():
    return 512


def select_columns(source, picks):
    width_all, source_cols = source.shape
    pick_count = picks.shape[0]
    block_size = block_length()
    block_count = pick_count // block_size
    pick_blocks = picks.reshape(block_count, block_size)
    source_rows = jnp.arange(source_cols, dtype=jnp.int32)[:, None]

    def select_per_block(entries):
        onehot_table = jnp.where(
            source_rows == entries[None, :], jnp.float32(1.0), jnp.float32(0.0)
        )
        return jnp.dot(
            source,
            onehot_table,
            precision=lax.Precision.HIGHEST,
            preferred_element_type=jnp.float32,
        )

    picked = lax.map(select_per_block, pick_blocks)
    return picked.transpose(1, 0, 2).reshape(width_all, pick_count)


def spread_cells(arrived, safe, scaled):
    width_all, slot_cols = arrived.shape
    entry_count, row_count, col_count = safe.shape
    block_size = block_length()
    entry_blocks = safe.transpose(1, 0, 2)
    weight_blocks = scaled.transpose(1, 0, 2)
    slot_rows = jnp.arange(slot_cols, dtype=jnp.int32)[:, None]

    def spread_per_block(pair):
        entries, weights_k = pair
        onehot_table = jnp.zeros((slot_cols, block_size), jnp.float32)
        for k in range(entry_count):
            onehot_table = onehot_table + jnp.where(
                slot_rows == entries[k][None, :], weights_k[k][None, :], jnp.float32(0.0)
            )
        return jnp.dot(
            arrived,
            onehot_table,
            precision=lax.Precision.HIGHEST,
            preferred_element_type=jnp.float32,
        )

    spread = lax.map(spread_per_block, (entry_blocks, weight_blocks))
    return spread.transpose(1, 0, 2)


def local(
    mode_shapes,
    send_nodes,
    interp_index,
    interp_weight,
    blend,
    motion_gain,
    frequency,
    volume,
    jacobian,
    state,
):
    outgoing = select_columns(mode_shapes, send_nodes[0])
    arrived = lax.all_to_all(outgoing, ("group", "dom"), split_axis=1, concat_axis=1, tiled=True)
    rows = blend.shape[0]
    cols = blend.shape[1]
    live = interp_index >= 0
    safe = jnp.maximum(interp_index, 0)
    weight = jnp.where(live, interp_weight, jnp.float32(0.0))
    scaled = weight * (blend / jnp.sum(weight, axis=0))[None]
    motion = spread_cells(arrived, safe, scaled)
    gain = motion_gain.reshape(2, VARS, COMP, rows, cols)
    disp = motion.reshape(CASES, COMP, rows, cols)
    pos_force = jnp.zeros((CASES, VARS, rows, cols), jnp.float32)
    vel_force = jnp.zeros((CASES, VARS, rows, cols), jnp.float32)
    for x in range(COMP):
        pos_force = pos_force + gain[0, :, x][None] * disp[:, x][:, None]
        vel_force = vel_force + gain[1, :, x][None] * disp[:, x][:, None]
    blocks = jacobian.reshape(5, VARS, VARS, rows, cols)
    field = state.reshape(CASES, 2, VARS, rows, cols)
    omega = frequency[:, None, None, None]
    padded = extended(state, (("group", 1), ("dom", 2)), 1)
    wide = padded.reshape(CASES, 2, VARS, rows + 2, cols + 2)
    flux = apply_block(blocks[0], field)
    flux = flux + apply_block(blocks[1], wide[:, :, :, :-2, 1:-1])
    flux = flux + apply_block(blocks[2], wide[:, :, :, 2:, 1:-1])
    flux = flux + apply_block(blocks[3], wide[:, :, :, 1:-1, :-2])
    flux = flux + apply_block(blocks[4], wide[:, :, :, 1:-1, 2:])
    real_field = field[:, 0].astype(jnp.float32)
    imag_field = field[:, 1].astype(jnp.float32)
    real_part = flux[:, 0] - omega * volume[None, None] * imag_field + pos_force
    imag_part = flux[:, 1] + omega * volume[None, None] * real_field + omega * vel_force
    residual = jnp.stack([real_part, imag_part], axis=1).reshape(CASES * 2 * VARS, rows, cols)
    return (motion, residual)


def solution(mesh):
    placed = (
        P(None, ("group", "dom")),
        P(("group", "dom"), None),
        P(None, "group", "dom"),
        P(None, "group", "dom"),
        P("group", "dom"),
        P(None, "group", "dom"),
        P(),
        P("group", "dom"),
        P(None, "group", "dom"),
        P(None, "group", "dom"),
    )
    return jax.shard_map(
        local,
        mesh=mesh,
        in_specs=placed,
        out_specs=(P(None, "group", "dom"), P(None, "group", "dom")),
        check_vma=False,
    )
```

profile of v0, /device:TPU:0, one launch (start us, length us, event | category | flops | bytes accessed | tf_op | source)
XLA Modules:
  0.0 362.3 jit_solution(6113102965215877448)
XLA Ops:
  0.6 3.5 fusion.82
  4.9 5.6 %collective-permute-start = (bf16[320,1,512]{2,0,1:T(8,128)(2,1)}, bf16[320,1,512]{2,0,1:T(8,128)(2,1)}, u32[]{:S(2)}, u32[]{:S(2)}) collective-permute-start(bf16[320,1,512]{2,0,1:T(8,128)(2,1)} %copy.67), channel_id=1, source_target_pairs={{0,8},{8,16},{16,24},{1,9},{9,17},{17,25},{2,10},{10,18},{18,26},{... | collective-permute-start | bytes 983048 | tf_op jit(solution)/shard_map/ppermute | solution.py:18
  11.3 1.3 collective-permute-start.1
  13.1 1.3 reduce.3
  14.4 8.4 %while.23 = (s32[]{:T(128)}, f32[2,96,512]{2,1,0:T(8,128)S(1)}, s32[2,512]{1,0:T(2,128)S(1)}, f32[96,2048]{1,0:T(8,128)}, s32[]{:T(128)}) while((s32[]{:T(128)}, f32[2,96,512]{2,1,0:T(8,128)S(1)}, s32[2,512]{1,0:T(2,128)S(1)}, f32[96,2048]{1,0:T(8,128)}, s32[]{:T(128)}) %tuple.131), condition=%wide.region_2.3_spmd.clone, body=%wide.region_1.2_spmd.clone.sunk | while | flops 1210056704 | bytes 989253 | solution.py:54
  14.5 4.2 %fusion.94 = f32[2,96,512]{2,1,0:T(8,128)S(1)} fusion(f32[2,96,512]{2,1,0:T(8,128)S(1)} %get-tuple-element.350, s32[]{:T(128)} %get-tuple-element.349, f32[96,2048]{1,0:T(8,128)} %get-tuple-element.357, s32[512]{0:T(512)S(1)} %bitcast.315), kind=kOutput, calls=%fused_computation.9.clone.1 | convolution fusion | flops 1210056704 | bytes 985092 | tf_op jit(solution)/shard_map/while/body/eval_jaxpr/dot_general | solution.py:47
  18.7 4.2 %fusion.94 = f32[2,96,512]{2,1,0:T(8,128)S(1)} fusion(f32[2,96,512]{2,1,0:T(8,128)S(1)} %get-tuple-element.350, s32[]{:T(128)} %get-tuple-element.349, f32[96,2048]{1,0:T(8,128)} %get-tuple-element.357, s32[512]{0:T(512)S(1)} %bitcast.315), kind=kOutput, calls=%fused_computation.9.clone.1 | convolution fusion | flops 1210056704 | bytes 985092 | tf_op jit(solution)/shard_map/while/body/eval_jaxpr/dot_general | solution.py:47
  23.9 7.1 %all-to-all-start = ((f32[96,32,32]{0,2,1:T(8,128)}), f32[96,32,32]{0,2,1:T(8,128)}, u32[]{:S(2)}, u32[]{:S(2)}) async-start(f32[96,32,32]{0,2,1:T(8,128)} %bitcast.3), calls=%async_computation | async-start | bytes 1048576 | tf_op jit(solution)/shard_map/all_to_all | solution.py:97
  31.0 4.1 %fusion.83 = (f32[25,16,512]{2,1,0:T(8,128)S(1)}, f32[25,16,512]{2,1,0:T(8,128)S(1)}, f32[25,16,512]{2,1,0:T(8,128)S(1)}, f32[25,16,512]{2,1,0:T(8,128)}, f32[25,16,512]{2,1,0:T(8,128)}) fusion(f32[125,16,512]{2,1,0:T(8,128)} %param.22), kind=kLoop, calls=%fused_computation.172 | loop fusion | bytes 8192000 | tf_op jit(solution)/shard_map/slice | solution.py:117
  36.1 4.1 %fusion.80 = (f32[32,2,16,512]{3,2,1,0:T(8,128)S(1)}, f32[32,2,16,512]{3,2,1,0:T(8,128)}, f32[32,2,16,512]{3,2,1,0:T(8,128)}, f32[32,2,16,512]{3,2,1,0:T(8,128)}, f32[32,2,16,512]{3,2,1,0:T(8,128)}) fusion(bf16[32,2,5,16,512]{4,3,2,1,0:T(8,128)(2,1)S(1)} %bitcast.289), kind=kLoop, calls=%fused_computation.131 | loop fusion | flops 2621440 | bytes 15728640 | tf_op jit(solution)/shard_map/mul | solution.py:27
  41.2 1.1 slice_bitcast_fusion.48
  42.8 1.1 broadcast_multiply_fusion
  44.9 9.6 %copy.62 = bf16[320,16,512]{0,1,2:T(8,128)(2,1)} copy(bf16[320,16,512]{2,1,0:T(8,128)(2,1)} %param.23) | data formatting | bytes 10485760 | tf_op args[9]
  54.5 2.4 slice_bitcast_fusion.38
  56.9 2.4 copy.61
  59.4 2.9 copy.63
  63.0 2.1 collective-permute-start.2
  65.1 1.5 collective-permute-start.3
  67.5 1.9 collective-permute-done.3
  69.3 12.4 %pad_maximum_fusion.1 = bf16[320,18,514]{0,1,2:T(8,128)(2,1)} fusion(bf16[320,18,1]{0,1,2:T(8,128)(2,1)S(1)} %collective-permute-done.3, bf16[320,1,512]{0,1,2:T(2,128)(2,1)} %copy.63, bf16[320,16,512]{0,1,2:T(8,128)(2,1)} %copy.62, bf16[320,1,512]{0,1,2:T(2,128)(2,1)S(1)} %copy.61, bf16[320,18,1]{0,1,2:T(8,128)(2,1)S(1)} %collective-permute-done.2), kind=kLoop, calls=%fused_computation.74 | loop fusion | flops 29606400 | bytes 11842560 | tf_op jit(solution)/shard_map/concatenate | solution.py:20
  81.7 15.6 %copy.64 = bf16[320,18,514]{2,1,0:T(8,128)(2,1)} copy(bf16[320,18,514]{0,1,2:T(8,128)(2,1)} %pad_maximum_fusion.1) | data formatting | bytes 11842560 | tf_op jit(solution)/shard_map/concatenate | solution.py:20
  97.4 29.8 %fusion.75 = (f32[32,2,16,512]{3,2,1,0:T(8,128)}, f32[32,2,16,512]{3,2,1,0:T(8,128)}, f32[32,2,16,512]{3,2,1,0:T(8,128)}, f32[32,2,16,512]{3,2,1,0:T(8,128)}, f3...) fusion(bf16[32,2,5,18,514]{4,3,2,1,0:T(8,128)(2,1)} %bitcast.284), kind=kLoop, calls=%fused_computation.121 | loop fusion | flops 9961472 | bytes 59768832 | tf_op jit(solution)/shard_map/mul | solution.py:27
  127.2 3.0 fusion.74
  130.3 42.9 %add_add_fusion = f32[32,2,5,16,512]{4,3,2,1,0:T(8,128)} fusion(f32[32,2,16,512]{3,2,1,0:T(8,128)} %get-tuple-element.180, f32[5,16,512]{2,1,0:T(8,128)} %get-tuple-element.242, f32[32,2,16,512]{3,2,1,0:T(8,128)} %get-tuple-element.181, f32[5,16,512]{2,1,0:T(8,128)} %get-tuple-element.243, f32[32,2,16,512]{3,2,1,0:T(8,128)} %get-tuple-element.182, ...), kind=kLoop, calls=%fused_computation.73 | loop fusion | flops 128450560 | bytes 67010560 | tf_op jit(solution)/shard_map/add | solution.py:121
  173.2 1.2 copy.57
  174.5 172.3 %while.24 = (s32[]{:T(128)}, f32[16,96,512]{2,0,1:T(8,128)}, s32[16,8,512]{2,1,0:T(8,128)}, f32[16,8,512]{2,1,0:T(8,128)}, f32[96,1024]{1,0:T(8,128)S(1)}, /*ind...) while((s32[]{:T(128)}, f32[16,96,512]{2,0,1:T(8,128)}, ...), condition=%wide.region_4.5_spmd.clone.clone, body=%wide.region_3.4_spmd.clone.clone.sunk | while | flops 616038400 | bytes 1474845 | solution.py:80
  176.8 3.4 fusion.97
  180.4 5.0 %dynamic_update_slice.15 = f32[16,96,512]{2,0,1:T(8,128)} dynamic-update-slice(f32[16,96,512]{2,0,1:T(8,128)} %get-tuple-element.374, f32[1,96,512]{2,0,1:T(1,128)S(1)} %copy.82, s32[]{:T(128)} %get-tuple-element.373, s32[]{:T(128)} %constant.21.clone.1..sunk, s32[]{:T(128)} %constant.21.clone.1..sunk) | dynamic-update-slice | bytes 393220 | tf_op jit(solution)/shard_map/while/body/jit(dynamic_update_index_in_dim)/dynamic_update_slice | solution.py:80
  187.5 3.4 fusion.97
  191.2 5.0 %dynamic_update_slice.15 = f32[16,96,512]{2,0,1:T(8,128)} dynamic-update-slice(f32[16,96,512]{2,0,1:T(8,128)} %get-tuple-element.374, f32[1,96,512]{2,0,1:T(1,128)S(1)} %copy.82, s32[]{:T(128)} %get-tuple-element.373, s32[]{:T(128)} %constant.21.clone.1..sunk, s32[]{:T(128)} %constant.21.clone.1..sunk) | dynamic-update-slice | bytes 393220 | tf_op jit(solution)/shard_map/while/body/jit(dynamic_update_index_in_dim)/dynamic_update_slice | solution.py:80
  198.3 3.4 fusion.97
  201.9 5.0 %dynamic_update_slice.15 = f32[16,96,512]{2,0,1:T(8,128)} dynamic-update-slice(f32[16,96,512]{2,0,1:T(8,128)} %get-tuple-element.374, f32[1,96,512]{2,0,1:T(1,128)S(1)} %copy.82, s32[]{:T(128)} %get-tuple-element.373, s32[]{:T(128)} %constant.21.clone.1..sunk, s32[]{:T(128)} %constant.21.clone.1..sunk) | dynamic-update-slice | bytes 393220 | tf_op jit(solution)/shard_map/while/body/jit(dynamic_update_index_in_dim)/dynamic_update_slice | solution.py:80
  208.0 1.0 constant_dynamic-slice_fusion.22
  209.0 3.4 fusion.97
  212.6 5.0 %dynamic_update_slice.15 = f32[16,96,512]{2,0,1:T(8,128)} dynamic-update-slice(f32[16,96,512]{2,0,1:T(8,128)} %get-tuple-element.374, f32[1,96,512]{2,0,1:T(1,128)S(1)} %copy.82, s32[]{:T(128)} %get-tuple-element.373, s32[]{:T(128)} %constant.21.clone.1..sunk, s32[]{:T(128)} %constant.21.clone.1..sunk) | dynamic-update-slice | bytes 393220 | tf_op jit(solution)/shard_map/while/body/jit(dynamic_update_index_in_dim)/dynamic_update_slice | solution.py:80
  219.7 3.4 fusion.97
  223.4 5.0 %dynamic_update_slice.15 = f32[16,96,512]{2,0,1:T(8,128)} dynamic-update-slice(f32[16,96,512]{2,0,1:T(8,128)} %get-tuple-element.374, f32[1,96,512]{2,0,1:T(1,128)S(1)} %copy.82, s32[]{:T(128)} %get-tuple-element.373, s32[]{:T(128)} %constant.21.clone.1..sunk, s32[]{:T(128)} %constant.21.clone.1..sunk) | dynamic-update-slice | bytes 393220 | tf_op jit(solution)/shard_map/while/body/jit(dynamic_update_index_in_dim)/dynamic_update_slice | solution.py:80
  230.5 3.4 fusion.97
  234.1 5.0 %dynamic_update_slice.15 = f32[16,96,512]{2,0,1:T(8,128)} dynamic-update-slice(f32[16,96,512]{2,0,1:T(8,128)} %get-tuple-element.374, f32[1,96,512]{2,0,1:T(1,128)S(1)} %copy.82, s32[]{:T(128)} %get-tuple-element.373, s32[]{:T(128)} %constant.21.clone.1..sunk, s32[]{:T(128)} %constant.21.clone.1..sunk) | dynamic-update-slice | bytes 393220 | tf_op jit(solution)/shard_map/while/body/jit(dynamic_update_index_in_dim)/dynamic_update_slice | solution.py:80
  241.2 3.4 fusion.97
  244.9 5.0 %dynamic_update_slice.15 = f32[16,96,512]{2,0,1:T(8,128)} dynamic-update-slice(f32[16,96,512]{2,0,1:T(8,128)} %get-tuple-element.374, f32[1,96,512]{2,0,1:T(1,128)S(1)} %copy.82, s32[]{:T(128)} %get-tuple-element.373, s32[]{:T(128)} %constant.21.clone.1..sunk, s32[]{:T(128)} %constant.21.clone.1..sunk) | dynamic-update-slice | bytes 393220 | tf_op jit(solution)/shard_map/while/body/jit(dynamic_update_index_in_dim)/dynamic_update_slice | solution.py:80
  250.9 1.0 constant_dynamic-slice_fusion.22
  252.0 3.4 fusion.97
  255.6 5.0 %dynamic_update_slice.15 = f32[16,96,512]{2,0,1:T(8,128)} dynamic-update-slice(f32[16,96,512]{2,0,1:T(8,128)} %get-tuple-element.374, f32[1,96,512]{2,0,1:T(1,128)S(1)} %copy.82, s32[]{:T(128)} %get-tuple-element.373, s32[]{:T(128)} %constant.21.clone.1..sunk, s32[]{:T(128)} %constant.21.clone.1..sunk) | dynamic-update-slice | bytes 393220 | tf_op jit(solution)/shard_map/while/body/jit(dynamic_update_index_in_dim)/dynamic_update_slice | solution.py:80
  262.7 3.4 fusion.97
  266.3 5.0 %dynamic_update_slice.15 = f32[16,96,512]{2,0,1:T(8,128)} dynamic-update-slice(f32[16,96,512]{2,0,1:T(8,128)} %get-tuple-element.374, f32[1,96,512]{2,0,1:T(1,128)S(1)} %copy.82, s32[]{:T(128)} %get-tuple-element.373, s32[]{:T(128)} %constant.21.clone.1..sunk, s32[]{:T(128)} %constant.21.clone.1..sunk) | dynamic-update-slice | bytes 393220 | tf_op jit(solution)/shard_map/while/body/jit(dynamic_update_index_in_dim)/dynamic_update_slice | solution.py:80
  273.4 3.4 fusion.97
  277.1 5.0 %dynamic_update_slice.15 = f32[16,96,512]{2,0,1:T(8,128)} dynamic-update-slice(f32[16,96,512]{2,0,1:T(8,128)} %get-tuple-element.374, f32[1,96,512]{2,0,1:T(1,128)S(1)} %copy.82, s32[]{:T(128)} %get-tuple-element.373, s32[]{:T(128)} %constant.21.clone.1..sunk, s32[]{:T(128)} %constant.21.clone.1..sunk) | dynamic-update-slice | bytes 393220 | tf_op jit(solution)/shard_map/while/body/jit(dynamic_update_index_in_dim)/dynamic_update_slice | solution.py:80
  284.2 3.4 fusion.97
  287.8 5.0 %dynamic_update_slice.15 = f32[16,96,512]{2,0,1:T(8,128)} dynamic-update-slice(f32[16,96,512]{2,0,1:T(8,128)} %get-tuple-element.374, f32[1,96,512]{2,0,1:T(1,128)S(1)} %copy.82, s32[]{:T(128)} %get-tuple-element.373, s32[]{:T(128)} %constant.21.clone.1..sunk, s32[]{:T(128)} %constant.21.clone.1..sunk) | dynamic-update-slice | bytes 393220 | tf_op jit(solution)/shard_map/while/body/jit(dynamic_update_index_in_dim)/dynamic_update_slice | solution.py:80
  294.9 3.4 fusion.97
  298.6 5.0 %dynamic_update_slice.15 = f32[16,96,512]{2,0,1:T(8,128)} dynamic-update-slice(f32[16,96,512]{2,0,1:T(8,128)} %get-tuple-element.374, f32[1,96,512]{2,0,1:T(1,128)S(1)} %copy.82, s32[]{:T(128)} %get-tuple-element.373, s32[]{:T(128)} %constant.21.clone.1..sunk, s32[]{:T(128)} %constant.21.clone.1..sunk) | dynamic-update-slice | bytes 393220 | tf_op jit(solution)/shard_map/while/body/jit(dynamic_update_index_in_dim)/dynamic_update_slice | solution.py:80
  304.6 1.3 constant_dynamic-slice_fusion.22
  305.9 3.4 fusion.97
  309.5 5.0 %dynamic_update_slice.15 = f32[16,96,512]{2,0,1:T(8,128)} dynamic-update-slice(f32[16,96,512]{2,0,1:T(8,128)} %get-tuple-element.374, f32[1,96,512]{2,0,1:T(1,128)S(1)} %copy.82, s32[]{:T(128)} %get-tuple-element.373, s32[]{:T(128)} %constant.21.clone.1..sunk, s32[]{:T(128)} %constant.21.clone.1..sunk) | dynamic-update-slice | bytes 393220 | tf_op jit(solution)/shard_map/while/body/jit(dynamic_update_index_in_dim)/dynamic_update_slice | solution.py:80
  316.6 3.4 fusion.97
  320.3 5.0 %dynamic_update_slice.15 = f32[16,96,512]{2,0,1:T(8,128)} dynamic-update-slice(f32[16,96,512]{2,0,1:T(8,128)} %get-tuple-element.374, f32[1,96,512]{2,0,1:T(1,128)S(1)} %copy.82, s32[]{:T(128)} %get-tuple-element.373, s32[]{:T(128)} %constant.21.clone.1..sunk, s32[]{:T(128)} %constant.21.clone.1..sunk) | dynamic-update-slice | bytes 393220 | tf_op jit(solution)/shard_map/while/body/jit(dynamic_update_index_in_dim)/dynamic_update_slice | solution.py:80
  327.4 3.4 fusion.97
  331.0 5.0 %dynamic_update_slice.15 = f32[16,96,512]{2,0,1:T(8,128)} dynamic-update-slice(f32[16,96,512]{2,0,1:T(8,128)} %get-tuple-element.374, f32[1,96,512]{2,0,1:T(1,128)S(1)} %copy.82, s32[]{:T(128)} %get-tuple-element.373, s32[]{:T(128)} %constant.21.clone.1..sunk, s32[]{:T(128)} %constant.21.clone.1..sunk) | dynamic-update-slice | bytes 393220 | tf_op jit(solution)/shard_map/while/body/jit(dynamic_update_index_in_dim)/dynamic_update_slice | solution.py:80
  338.1 3.4 fusion.97
  341.7 5.0 %dynamic_update_slice.15 = f32[16,96,512]{2,0,1:T(8,128)} dynamic-update-slice(f32[16,96,512]{2,0,1:T(8,128)} %get-tuple-element.374, f32[1,96,512]{2,0,1:T(1,128)S(1)} %copy.82, s32[]{:T(128)} %get-tuple-element.373, s32[]{:T(128)} %constant.21.clone.1..sunk, s32[]{:T(128)} %constant.21.clone.1..sunk) | dynamic-update-slice | bytes 393220 | tf_op jit(solution)/shard_map/while/body/jit(dynamic_update_index_in_dim)/dynamic_update_slice | solution.py:80
  346.8 2.3 slice_bitcast_fusion.2
  349.2 7.7 %fusion.55 = (f32[32,1,5,16,512]{4,3,2,1,0:T(8,128)S(1)}, f32[32,1,5,16,512]{4,3,2,1,0:T(8,128)S(1)}) fusion(f32[32,2,5,16,512]{4,3,2,1,0:T(8,128)} %add_add_fusion, bf16[32,2,5,16,512]{4,3,2,1,0:T(8,128)(2,1)} %bitcast.286, f32[32,16,512]{2,1,0:T(8,128)S(1)} %get-tuple-element.213, f32[5,16,512]{2,1,0:T(8,128)S(1)} %copy-done.16, ...), kind=kLoop, calls=%fused_computation.78 | loop fusion | flops 24903680 | bytes 31391872 | tf_op jit(solution)/shard_map/add | solution.py:124
  356.9 5.4 %pad_maximum_fusion = f32[32,2,5,16,512]{4,3,2,1,0:T(8,128)} fusion(f32[32,1,5,16,512]{4,3,2,1,0:T(8,128)S(1)} %get-tuple-element.178, f32[32,1,5,16,512]{4,3,2,1,0:T(8,128)S(1)} %get-tuple-element.177), kind=kLoop, calls=%fused_computation.72 | loop fusion | flops 2621440 | bytes 20971520 | tf_op jit(solution)/shard_map/stack | solution.py:126
  (112 shorter events, 41.3 us)
Async XLA Ops:
  4.9 52.0 %collective-permute-start = (bf16[320,1,512]{2,0,1:T(8,128)(2,1)}, bf16[320,1,512]{2,0,1:T(8,128)(2,1)}, u32[]{:S(2)}, u32[]{:S(2)}) collective-permute-start(bf16[320,1,512]{2,0,1:T(8,128)(2,1)} %copy.67), channel_id=1, source_target_pairs={{0,8},{8,16},{16,24},{1,9},{9,17},{17,25},{2,10},{10,18},{18,26},{... | collective-permute-start | bytes 983048 | tf_op jit(solution)/shard_map/ppermute | solution.py:18
  11.3 48.1 %collective-permute-start.1 = (bf16[320,1,512]{2,0,1:T(8,128)(2,1)}, bf16[320,1,512]{2,0,1:T(8,128)(2,1)}, u32[]{:S(2)}, u32[]{:S(2)}) collective-permute-start(bf16[320,1,512]{2,0,1:T(8,128)(2,1)} %copy.68), channel_id=1, source_target_pairs={{8,0},{16,8},{24,16},{9,1},{17,9},{25,17},{10,2},{18,10},{26,18},{... | collective-permute-start | bytes 983048 | tf_op jit(solution)/shard_map/ppermute | solution.py:19
  23.9 12.2 %slice-start = ((s8[5242880]{0:T(1024)(128)(4,1)}), s8[1048576]{0:T(1024)(128)(4,1)S(1)}, s32[]{:S(2)}) async-start(s8[5242880]{0:T(1024)(128)(4,1)} %bitcast.287), calls=%async_computation.1 | async-start | bytes 2097152
  23.9 149.4 %all-to-all-start = ((f32[96,32,32]{0,2,1:T(8,128)}), f32[96,32,32]{0,2,1:T(8,128)}, u32[]{:S(2)}, u32[]{:S(2)}) async-start(f32[96,32,32]{0,2,1:T(8,128)} %bitcast.3), calls=%async_computation | async-start | bytes 1048576 | tf_op jit(solution)/shard_map/all_to_all | solution.py:97
  31.0 5.1 %slice-start.1 = ((s8[5242880]{0:T(1024)(128)(4,1)}), s8[4194304]{0:T(1024)(128)(4,1)S(1)}, s32[]{:S(2)}) async-start(s8[5242880]{0:T(1024)(128)(4,1)} %bitcast.287), calls=%async_computation.2 | async-start | bytes 8388608
  36.1 4.2 %copy-start.4 = (f32[30,16,512]{2,1,0:T(8,128)S(1)}, f32[30,16,512]{2,1,0:T(8,128)}, u32[]{:S(2)}) copy-start(f32[30,16,512]{2,1,0:T(8,128)} %param.19) | copy-start | bytes 2949124
  40.2 2.2 copy-start.2
  40.2 2.2 copy-start.3
  40.2 2.5 copy-start.18
  40.2 2.6 copy-start.19
  40.2 2.6 copy-start.20
  44.9 9.6 %copy-start.1 = (f32[25,16,512]{2,1,0:T(8,128)S(1)}, f32[25,16,512]{2,1,0:T(8,128)}, u32[]{:S(2)}) copy-start(f32[25,16,512]{2,1,0:T(8,128)} %get-tuple-element.210) | copy-start | bytes 2457604
  63.0 4.5 %collective-permute-start.2 = (bf16[320,18,1]{0,1,2:T(8,128)(2,1)S(1)}, bf16[320,18,1]{0,1,2:T(8,128)(2,1)S(1)}, u32[]{:S(2)}, u32[]{:S(2)}) collective-permute-start(bf16[320,18,1]{0,1,2:T(8,128)(2,1)S(1)} %get-tuple-element.198), channel_id=1, source_target_pairs={{0,1},{1,2},{2,3},{3,4},{4,5},{5,6},{6,7},{8,9},{9,10},{10,11},{11... | collective-permute-start | bytes 34568 | tf_op jit(solution)/shard_map/ppermute | solution.py:18
  65.1 4.2 %collective-permute-start.3 = (bf16[320,18,1]{0,1,2:T(8,128)(2,1)S(1)}, bf16[320,18,1]{0,1,2:T(8,128)(2,1)S(1)}, u32[]{:S(2)}, u32[]{:S(2)}) collective-permute-start(bf16[320,18,1]{0,1,2:T(8,128)(2,1)S(1)} %get-tuple-element.199), channel_id=1, source_target_pairs={{1,0},{2,1},{3,2},{4,3},{5,4},{6,5},{7,6},{9,8},{10,9},{11,10},{12... | collective-permute-start | bytes 34568 | tf_op jit(solution)/shard_map/ppermute | solution.py:19
  97.3 32.9 %copy-start.5 = (f32[5,16,512]{2,1,0:T(8,128)S(1)}, f32[5,16,512]{2,1,0:T(8,128)}, u32[]{:S(2)}) copy-start(f32[5,16,512]{2,1,0:T(8,128)} %get-tuple-element.232) | copy-start | bytes 491524
  97.3 32.9 %copy-start.6 = (f32[5,16,512]{2,1,0:T(8,128)S(1)}, f32[5,16,512]{2,1,0:T(8,128)}, u32[]{:S(2)}) copy-start(f32[5,16,512]{2,1,0:T(8,128)} %get-tuple-element.233) | copy-start | bytes 491524
  97.3 32.9 %copy-start.7 = (f32[5,16,512]{2,1,0:T(8,128)S(1)}, f32[5,16,512]{2,1,0:T(8,128)}, u32[]{:S(2)}) copy-start(f32[5,16,512]{2,1,0:T(8,128)} %get-tuple-element.234) | copy-start | bytes 491524
  97.4 32.9 %copy-start.8 = (f32[5,16,512]{2,1,0:T(8,128)S(1)}, f32[5,16,512]{2,1,0:T(8,128)}, u32[]{:S(2)}) copy-start(f32[5,16,512]{2,1,0:T(8,128)} %get-tuple-element.235) | copy-start | bytes 491524
  97.4 32.9 %copy-start.9 = (f32[5,16,512]{2,1,0:T(8,128)S(1)}, f32[5,16,512]{2,1,0:T(8,128)}, u32[]{:S(2)}) copy-start(f32[5,16,512]{2,1,0:T(8,128)} %get-tuple-element.251) | copy-start | bytes 491524
  97.4 32.9 %copy-start.10 = (f32[5,16,512]{2,1,0:T(8,128)S(1)}, f32[5,16,512]{2,1,0:T(8,128)}, u32[]{:S(2)}) copy-start(f32[5,16,512]{2,1,0:T(8,128)} %get-tuple-element.252) | copy-start | bytes 491524
  97.4 32.9 %copy-start.11 = (f32[5,16,512]{2,1,0:T(8,128)S(1)}, f32[5,16,512]{2,1,0:T(8,128)}, u32[]{:S(2)}) copy-start(f32[5,16,512]{2,1,0:T(8,128)} %get-tuple-element.253) | copy-start | bytes 491524
  346.8 2.4 copy-start
  346.8 2.4 copy-start.12
  346.8 2.4 copy-start.13
  346.8 2.4 copy-start.14
  346.8 2.4 copy-start.15
  346.8 2.4 copy-start.16
  346.8 2.4 copy-start.17
where the time goes:
time: 370 us; the launch traced here: 362 us
  local copies, waits for them, and re-layouts  167 us (45%)
  other arithmetic  111 us (30%)
  matrix products  63 us (17%)
  starting transfers between devices  17.5 us (5%)
    dynamic_update_slice x32, local copies, waits for them, and re-layouts, spread_cells(): spread = lax.map(spread_per_block, (entry_blocks, weight_blocks))  83.8 us
    dot_general x16, matrix products, spread_per_block(): jnp.dot(arrived, onehot_table, precision=lax.Precision.HIGHEST, preferred...  54.6 us
    add x1, other arithmetic, local(): flux = flux + apply_block(blocks[4], wide[:, :, :, 1:-1, 2:])  42.9 us
    mul x3, other arithmetic, apply_block(): block[:, u][None, None] * field[:, :, u][:, :, None].astype(jnp.float32)  37 us
    slice x16, local copies, waits for them, and re-layouts, spread_per_block(): entries[k][None, :]  16.9 us
    slice x16, local copies, waits for them, and re-layouts, spread_per_block(): weights_k[k][None, :]  16.4 us
    concatenate x1, local copies, waits for them, and re-layouts, extended(): value = jnp.concatenate([before, value, after], axis=dim)  15.6 us
    unnamed x51, local copies, waits for them, and re-layouts  12.9 us
  transfers between devices with their start and end apart: 5, of which 1 were waited for; matrix products, arithmetic and copies ran while one was open for 41% of the time, Pallas kernels for 0%

commit v1 on v0

v1 whole, which is shorter than its diff:
```python
import functools
import jax
import jax.numpy as jnp
from jax import lax
from jax.experimental import pallas as pl
from jax.experimental.pallas import tpu as pltpu
from jax.sharding import PartitionSpec as P

COMP = 3
VARS = 5
PARTS = 2
LANES = 128
SUB = 8
F32 = jnp.float32
BF16 = jnp.bfloat16


def halves(value):
    hi = value.astype(BF16)
    lo = (value - hi.astype(F32)).astype(BF16)
    return hi, lo


def diagonal(rows, cols, offset):
    r = lax.broadcasted_iota(jnp.int32, (rows, cols), 0)
    c = lax.broadcasted_iota(jnp.int32, (rows, cols), 1)
    return jnp.where(r + offset == c, 1.0, 0.0).astype(BF16)


def outgoing_kernel(modes, nodes, state, table, top, bottom, first, last, split, picked):
    width, owned = modes.shape
    planes, rows, cols = state.shape
    listed = nodes.shape[1]

    @pl.when(pl.program_id(0) == 0)
    def _():
        hi, lo = halves(modes[...])
        split[0:width] = hi
        split[width:] = lo
        step = min(listed, 256)
        node_rows = lax.broadcasted_iota(jnp.int32, (owned, step), 0)

        def pick(b, _):
            at = pl.ds(pl.multiple_of(b * step, step), step)
            onehot = jnp.where(node_rows == nodes[:, at], 1.0, 0.0).astype(BF16)
            picked[...] = jnp.dot(split[...], onehot, preferred_element_type=F32)
            table[at, :] = picked[...].T.astype(BF16)
            return 0

        lax.fori_loop(0, listed // step, pick, 0)

    r = lax.broadcasted_iota(jnp.int32, (32, 16 * rows), 0)
    c = lax.broadcasted_iota(jnp.int32, (32, 16 * rows), 1)
    want = jnp.where(r < 16, r * rows, (r - 16) * rows + rows - 1)
    faces = jnp.where(c == want, 1.0, 0.0).astype(BF16)
    for g in range(planes // 16):
        block = state[g * 16 : g * 16 + 16].reshape(16 * rows, cols)
        got = jnp.dot(faces, block, preferred_element_type=F32).astype(BF16)
        top[g * 16 : g * 16 + 16, :] = got[0:16]
        bottom[g * 16 : g * 16 + 16, :] = got[16:32]
    er = lax.broadcasted_iota(jnp.int32, (SUB, LANES), 0)
    ec = lax.broadcasted_iota(jnp.int32, (SUB, LANES), 1)
    nt = (((1,), (1,)), ((), ()))
    pick_first = jnp.where(ec == 0, 1.0, 0.0).astype(BF16)
    pick_last = jnp.where(ec == LANES - 1, 1.0, 0.0).astype(BF16)
    left = state[:, :, 0:LANES].reshape(planes * rows, LANES)
    right = state[:, :, cols - LANES : cols].reshape(planes * rows, LANES)
    first[0] = lax.dot_general(pick_first, left, nt, preferred_element_type=F32)[0:1]
    last[0] = lax.dot_general(pick_last, right, nt, preferred_element_type=F32)[0:1]


def outgoing(modes, nodes, state):
    width, owned = modes.shape
    listed = nodes.shape[1]
    n, rows, cols = state.shape
    steps = 4
    planes = n // steps
    whole = lambda g: (0, 0)
    return pl.pallas_call(
        outgoing_kernel,
        grid=(steps,),
        in_specs=[
            pl.BlockSpec((width, owned), whole),
            pl.BlockSpec((1, listed), whole),
            pl.BlockSpec((planes, rows, cols), lambda g: (g, 0, 0)),
        ],
        out_specs=[
            pl.BlockSpec((listed, 2 * width), whole),
            pl.BlockSpec((planes, cols), lambda g: (g, 0)),
            pl.BlockSpec((planes, cols), lambda g: (g, 0)),
            pl.BlockSpec((1, 1, planes * rows), lambda g: (g, 0, 0)),
            pl.BlockSpec((1, 1, planes * rows), lambda g: (g, 0, 0)),
        ],
        out_shape=[
            jax.ShapeDtypeStruct((listed, 2 * width), BF16),
            jax.ShapeDtypeStruct((n, cols), BF16),
            jax.ShapeDtypeStruct((n, cols), BF16),
            jax.ShapeDtypeStruct((steps, 1, planes * rows), F32),
            jax.ShapeDtypeStruct((steps, 1, planes * rows), F32),
        ],
        scratch_shapes=[
            pltpu.VMEM((2 * width, owned), BF16),
            pltpu.VMEM((2 * width, min(listed, 256)), F32),
        ],
        compiler_params=pltpu.CompilerParams(vmem_limit_bytes=24 << 20),
    )(modes, nodes, state)


def inner_kernel(fields, jac, state, out, coef, centre, before, after):
    planes, rows, cols = state.shape
    blocks = cols // LANES
    high = rows // SUB

    @pl.when(pl.program_id(0) == 0)
    def _():
        for d, source in enumerate((0, 3, 4)):
            for m in range(VARS * VARS):
                for b in range(blocks):
                    for h in range(high):
                        coef[b * high + h, d * VARS * VARS + m] = jac[
                            source * VARS * VARS + m, h * SUB : h * SUB + SUB, b * LANES : b * LANES + LANES
                        ]

    flat = state[...].reshape(planes * rows, cols)
    shape = (planes, high, SUB, LANES)
    prior = jnp.dot(flat, diagonal(cols, cols, 1), preferred_element_type=F32)
    later = jnp.dot(flat, diagonal(cols, cols, -1), preferred_element_type=F32)
    here = state[...].astype(F32).reshape(planes * rows, cols)
    for b in range(blocks):
        at = slice(b * LANES, b * LANES + LANES)
        centre[b] = here[:, at].reshape(shape)
        before[b] = prior[:, at].reshape(shape)
        after[b] = later[:, at].reshape(shape)
    groups = planes // (fields * VARS)

    for b in range(blocks):
        kinds = [(0, centre)]
        if b > 0:
            kinds.append((1, before))
        if b < blocks - 1:
            kinds.append((2, after))

        def body(t, _, b=b, kinds=kinds):
            g = t // high
            h = t % high
            at = pl.ds(pl.multiple_of(h * SUB, SUB), SUB)
            acc = [[None] * VARS for _ in range(fields)]
            for d, source in kinds:
                for u in range(VARS):
                    q = [source[b, g * fields * VARS + f * VARS + u, h] for f in range(fields)]
                    for v in range(VARS):
                        j = coef[b * high + h, d * VARS * VARS + v * VARS + u]
                        for f in range(fields):
                            term = j * q[f]
                            acc[f][v] = term if acc[f][v] is None else acc[f][v] + term
            for f in range(fields):
                for v in range(VARS):
                    out[g * fields * VARS + f * VARS + v, at, b * LANES : b * LANES + LANES] = acc[f][v]
            return 0

        lax.fori_loop(0, groups * high, body, 0)


def inner_flux(jac, state):
    n, rows, cols = state.shape
    blocks = cols // LANES
    high = rows // SUB
    fields = 8
    planes = fields * VARS
    hold = pltpu.VMEM((blocks, planes, high, SUB, LANES), F32)
    return pl.pallas_call(
        functools.partial(inner_kernel, fields),
        grid=(n // planes,),
        in_specs=[
            pl.BlockSpec(jac.shape, lambda g: (0, 0, 0), pipeline_mode=pl.Buffered(1)),
            pl.BlockSpec((planes, rows, cols), lambda g: (g, 0, 0)),
        ],
        out_specs=pl.BlockSpec((planes, rows, cols), lambda g: (g, 0, 0)),
        out_shape=jax.ShapeDtypeStruct((n, rows, cols), F32),
        scratch_shapes=[pltpu.VMEM((blocks * high, 3 * VARS * VARS, SUB, LANES), F32), hold, hold, hold],
        compiler_params=pltpu.CompilerParams(vmem_limit_bytes=40 << 20),
        cost_estimate=pl.CostEstimate(flops=40_000_000_000, bytes_accessed=60_000_000, transcendentals=0),
    )(jac, state)


def outer_kernel(
    edge, freq, table, index, weight, blend, gain, volume, lower, upper, before, after, state,
    above, below, left, right, partial, motion, residual,
    modes, wide, side, shares, keys, w_hi, w_lo, moved,
):
    n, rows, _ = state.shape
    high = rows // SUB
    slots, width2 = table.shape
    width = width2 // 2
    entries = index.shape[0]
    cases = width // COMP
    jb = pl.program_id(0)
    blocks = pl.num_programs(0)

    @pl.when(jb == 0)
    def _():
        step = min(slots, 512)
        for b in range(slots // step):
            modes[:, b * step : b * step + step] = table[b * step : b * step + step, :].astype(F32).T.astype(BF16)

    live = [index[k] >= 0 for k in range(entries)]
    raw = [jnp.where(live[k], weight[k], 0.0) for k in range(entries)]
    total = raw[0]
    for k in range(1, entries):
        total = total + raw[k]
    scale = blend[...] / total
    share = [r * scale for r in raw]
    key = [index[k] for k in range(entries)]
    for k in range(entries):
        for m in range(k + 1, entries):
            same = key[k] == key[m]
            share[k] = jnp.where(same, share[k] + share[m], share[k])
            key[m] = jnp.where(same, -1, key[m])
    for k in range(entries):
        shares[k] = share[k]
        keys[k] = key[k]

    seg = 32
    slot_rows = lax.broadcasted_iota(jnp.int32, (seg, LANES), 0)

    def pair(i, _):
        for part in range(2):
            row = i * 2 + part
            at = slice(part * LANES, part * LANES + LANES)
            e = [jnp.broadcast_to(keys[k, pl.ds(row, 1), :], (SUB, LANES)) for k in range(entries)]
            w = [jnp.broadcast_to(shares[k, pl.ds(row, 1), :], (SUB, LANES)) for k in range(entries)]

            def build(s, _):
                base = pl.multiple_of(s * seg, seg)
                got = []
                for piece in range(seg // SUB):
                    ids = slot_rows[piece * SUB : piece * SUB + SUB] + base
                    value = jnp.where(ids == e[0], w[0], 0.0)
                    for k in range(1, entries):
                        value = jnp.where(ids == e[k], w[k], value)
                    got.append(value)
                hi, lo = halves(jnp.concatenate(got, axis=0))
                w_hi[pl.ds(base, seg), at] = hi
                w_lo[pl.ds(base, seg), at] = lo
                return 0

            lax.fori_loop(0, slots // seg, build, 0)
        both = jnp.dot(modes[...], w_hi[...], preferred_element_type=F32)
        rest = jnp.dot(modes[0:width, :], w_lo[...], preferred_element_type=F32)
        sums = both[0:width] + both[width:] + rest
        for part in range(2):
            at = slice(part * LANES, part * LANES + LANES)
            for c in range(width // SUB):
                moved[pl.ds(c * SUB * rows + i * 2 + part, SUB, stride=rows), :] = sums[c * SUB : c * SUB + SUB, at]
        return 0

    lax.fori_loop(0, rows // 2, pair, 0)
    for c in range(width):
        motion[c] = moved[c * rows : c * rows + rows, :]

    pitch = rows + 2 * SUB
    for p in range(n):
        wide[p * pitch + SUB : p * pitch + SUB + rows, :] = state[p].astype(F32)
    has_above = edge[0].astype(F32)
    has_below = edge[1].astype(F32)
    for g in range(n // 16):
        up = above[g * 16 : g * 16 + 16, :].astype(F32) * has_above
        down = below[g * 16 : g * 16 + 16, :].astype(F32) * has_below
        for half in range(2):
            start = (g * 16 + half * SUB) * pitch
            wide[pl.ds(start + SUB - 1, SUB, stride=pitch), :] = up[half * SUB : half * SUB + SUB]
            wide[pl.ds(start + SUB + rows, SUB, stride=pitch), :] = down[half * SUB : half * SUB + SUB]

    fields = 8
    lane = lax.broadcasted_iota(jnp.int32, (SUB, LANES), 1)

    def combine(extra):
        def body(t, _):
            g = t // high
            h = t % high
            at = pl.ds(pl.multiple_of(h * SUB, SUB), SUB)
            first = g * fields * VARS
            acc = [[partial[first + f * VARS + v, at, :] for v in range(VARS)] for f in range(fields)]
            for block, shift in ((lower, -1), (upper, 1)):
                for u in range(VARS):
                    q = [wide[pl.ds((first + f * VARS + u) * pitch + SUB + h * SUB + shift, SUB), :] for f in range(fields)]
                    for v in range(VARS):
                        j = block[v * VARS + u, at, :]
                        for f in range(fields):
                            acc[f][v] = acc[f][v] + j * q[f]
            if extra is not None:
                for u in range(VARS):
                    q = [side[first + f * VARS + u, at, :] for f in range(fields)]
                    for v in range(VARS):
                        j = extra[v * VARS + u, at, :]
                        for f in range(fields):
                            acc[f][v] = acc[f][v] + j * q[f]
            vol = volume[at, :]
            for c in range(fields // PARTS):
                case = g * (fields // PARTS) + c
                omega = freq[case]
                rate = vol * omega
                m = [moved[pl.ds((case * COMP + x) * rows + h * SUB, SUB), :] for x in range(COMP)]
                for v in range(VARS):
                    re = wide[pl.ds((first + c * 2 * VARS + v) * pitch + SUB + h * SUB, SUB), :]
                    im = wide[pl.ds((first + (c * 2 + 1) * VARS + v) * pitch + SUB + h * SUB, SUB), :]
                    pos = acc[2 * c][v] - rate * im
                    vel = gain[(VARS + v) * COMP, at, :] * m[0]
                    for x in range(COMP):
                        pos = pos + gain[v * COMP + x, at, :] * m[x]
                        if x > 0:
                            vel = vel + gain[(VARS + v) * COMP + x, at, :] * m[x]
                    residual[first + c * 2 * VARS + v, at, :] = pos
                    residual[first + (c * 2 + 1) * VARS + v, at, :] = acc[2 * c + 1][v] + rate * re + omega * vel
            return 0

        lax.fori_loop(0, n // (fields * VARS) * high, body, 0)

    def sideways(columns, flag, shift, edge_lane):
        steps, _, length = columns.shape
        group = LANES // rows
        for s in range(steps):
            for b in range(length // LANES):
                line = jnp.broadcast_to(columns[s, :, b * LANES : b * LANES + LANES] * flag, (SUB, LANES))
                stood = line.T
                for q in range(group):
                    p = (s * length + b * LANES) // rows + q
                    column = stood[q * rows : q * rows + rows, 0:1]
                    for h in range(high):
                        here = wide[p * pitch + SUB + h * SUB : p * pitch + SUB + h * SUB + SUB, :]
                        moved_over = pltpu.roll(here, shift, 1)
                        value = jnp.broadcast_to(column[h * SUB : h * SUB + SUB], (SUB, LANES))
                        side[p, h * SUB : h * SUB + SUB, :] = jnp.where(lane == edge_lane, value, moved_over)

    @pl.when(jb == 0)
    def _():
        sideways(left, edge[2].astype(F32), 1, 0)
        combine(before)

    @pl.when((jb > 0) & (jb < blocks - 1))
    def _():
        combine(None)

    @pl.when(jb == blocks - 1)
    def _():
        sideways(right, edge[3].astype(F32), LANES - 1, LANES - 1)
        combine(after)


def finish(edge, freq, table, index, weight, blend, gain, volume, jac, state, above, below, left, right, partial):
    n, rows, cols = state.shape
    slots, width2 = table.shape
    width = width2 // 2
    entries = index.shape[0]
    blocks = cols // LANES
    scalar = pl.BlockSpec(memory_space=pltpu.SMEM)
    cell3 = lambda lead: pl.BlockSpec((lead, rows, LANES), lambda b: (0, 0, b))
    cell2 = pl.BlockSpec((rows, LANES), lambda b: (0, b))
    jblock = lambda d: pl.BlockSpec((VARS * VARS, rows, LANES), lambda b: (d, 0, b))
    line = pl.BlockSpec((n, LANES), lambda b: (0, b))
    ends = pl.BlockSpec(left.shape, lambda b: (0, 0, 0))
    return pl.pallas_call(
        outer_kernel,
        grid=(blocks,),
        in_specs=[
            scalar, scalar,
            pl.BlockSpec(table.shape, lambda b: (0, 0)),
            cell3(entries), cell3(entries), cell2, cell3(gain.shape[0]), cell2,
            jblock(1), jblock(2), jblock(3), jblock(4),
            cell3(n), line, line, ends, ends, cell3(n),
        ],
        out_specs=[cell3(width), cell3(n)],
        out_shape=[
            jax.ShapeDtypeStruct((width, rows, cols), F32),
            jax.ShapeDtypeStruct((n, rows, cols), F32),
        ],
        scratch_shapes=[
            pltpu.VMEM((width2, slots), BF16),
            pltpu.VMEM((n * (rows + 2 * SUB), LANES), F32),
            pltpu.VMEM((n, rows, LANES), F32),
            pltpu.VMEM((entries, rows, LANES), F32),
            pltpu.VMEM((entries, rows, LANES), jnp.int32),
            pltpu.VMEM((slots, 2 * LANES), BF16),
            pltpu.VMEM((slots, 2 * LANES), BF16),
            pltpu.VMEM((width * rows, LANES), F32),
        ],
        compiler_params=pltpu.CompilerParams(vmem_limit_bytes=56 << 20),
    )(edge, freq, table, index, weight, blend, gain, volume, jac, jac, jac, jac, state, above, below, left, right, partial)


def ring(axis, step):
    peers = lax.axis_size(axis)
    return [(i, (i + step) % peers) for i in range(peers)]


def local(mode_shapes, send_nodes, interp_index, interp_weight, blend, motion_gain, frequency, volume, jacobian, state):
    axes = ("group", "dom")
    table, top, bottom, first, last = outgoing(mode_shapes, send_nodes, state)
    peers = lax.axis_size(axes)
    listed, width2 = table.shape
    arrived = lax.all_to_all(
        table.reshape(peers, listed // peers, width2), axes, split_axis=0, concat_axis=0, tiled=True
    ).reshape(listed, width2)
    above = lax.ppermute(bottom, "group", ring("group", 1))
    below = lax.ppermute(top, "group", ring("group", -1))
    left = lax.ppermute(last, "dom", ring("dom", 1))
    right = lax.ppermute(first, "dom", ring("dom", -1))
    gi, gn = lax.axis_index("group"), lax.axis_size("group")
    di, dn = lax.axis_index("dom"), lax.axis_size("dom")
    edge = jnp.stack([gi > 0, gi < gn - 1, di > 0, di < dn - 1]).astype(jnp.int32)
    partial = inner_flux(jacobian, state)
    return tuple(
        finish(
            edge, frequency, arrived, interp_index, interp_weight, blend, motion_gain, volume, jacobian, state,
            above, below, left, right, partial,
        )
    )


def solution(mesh):
    both = ("group", "dom")
    cells3 = P(None, "group", "dom")
    cells2 = P("group", "dom")
    placed = (P(None, both), P(both, None), cells3, cells3, cells2, cells3, P(), cells2, cells3, cells3)
    return jax.shard_map(local, mesh=mesh, in_specs=placed, out_specs=(cells3, cells3), check_vma=False)
```

time: 370 us -> 123 us (0.33); the launches traced: 362 us -> 122 us
  local copies, waits for them, and re-layouts: 167 us -> 9.92 us
  other arithmetic: 111 us -> 0.61 us
  Pallas kernels: 0 us -> 97.3 us
  matrix products: 63 us -> 0 us
    pallas_call x0 -> x3, Pallas kernels: none -> 97.3 us  [the longest x1 74.6 us: finish(): pl.pallas_call(outer_kernel, grid=(blocks,), in_specs=[scalar, scalar, pl...]
    dynamic_update_slice x32 -> x0, local copies, waits for them, and re-layouts: 83.8 us -> none  [spread_cells(): spread = lax.map(spread_per_block, (entry_blocks, weight_blocks))]
    dot_general x18 -> x0, matrix products: 63 us -> none  [the longest x16 54.6 us: spread_per_block(): jnp.dot(arrived, onehot_table, precision=lax.Precision.HIGHEST, preferred...]
    add x2 -> x0, other arithmetic: 50.6 us -> none  [the longest x1 42.9 us: local(): flux = flux + apply_block(blocks[4], wide[:, :, :, 1:-1, 2:])]
    slice x34 -> x0, local copies, waits for them, and re-layouts: 40.9 us -> none  [the longest x16 16.9 us: spread_per_block(): entries[k][None, :]]
    mul x4 -> x0, other arithmetic: 38.1 us -> none  [the longest x3 37 us: apply_block(): block[:, u][None, None] * field[:, :, u][:, :, None].astype(jnp.float32)]
    concatenate x1 -> x0, local copies, waits for them, and re-layouts: 15.6 us -> none  [extended(): value = jnp.concatenate([before, value, after], axis=dim)]
    concatenate x1 -> x0, other arithmetic: 12.4 us -> none  [extended(): value = jnp.concatenate([before, value, after], axis=dim)]
  transfers between devices with their start and end apart: 5 -> 5, of which waited for: 1 -> 0; matrix products, arithmetic and copies ran while one was open for 41% -> 1% of each run, Pallas kernels for 0% -> 15%
where the time goes in v1:
time: 123 us; the launch traced here: 122 us
  Pallas kernels  97.3 us (79%)
  starting transfers between devices  13.8 us (11%)
  local copies, waits for them, and re-layouts  9.92 us (8%)
    pallas_call x1, Pallas kernels, finish(): pl.pallas_call(outer_kernel, grid=(blocks,), in_specs=[scalar, scalar, pl...  74.6 us
    pallas_call x1, Pallas kernels, inner_flux(): pl.pallas_call(functools.partial(inner_kernel, fields), grid=(n // planes...  17.9 us
    unnamed x20, local copies, waits for them, and re-layouts  9.92 us
    all_to_all x1, starting transfers between devices, local(): lax.all_to_all(table.reshape(peers, listed // peers, width2), axes, split...  7.3 us
    pallas_call x1, Pallas kernels, outgoing(): pl.pallas_call(outgoing_kernel, grid=(steps,), in_specs=[pl.BlockSpec((wi...  4.76 us
    ppermute x1, starting transfers between devices, local(): right = lax.ppermute(first, 'dom', ring('dom', -1))  3.29 us
  transfers between devices with their start and end apart: 5, of which 0 were waited for; matrix products, arithmetic and copies ran while one was open for 1% of the time, Pallas kernels for 15%

profile of v1, /device:TPU:0, one launch (start us, length us, event | category | flops | bytes accessed | tf_op | source)
XLA Modules:
  0.0 122.3 jit_solution(5441422005227001132)
XLA Ops:
  0.6 0.0 copy-start.1
  0.6 2.5 %copy-done.1 = bf16[320,16,512]{2,1,0:T(8,128)(2,1)S(1)} copy-done((bf16[320,16,512]{2,1,0:T(8,128)(2,1)S(1)}, bf16[320,16,512]{2,1,0:T(8,128)(2,1)}, u32[]{:S(2)}) %copy-start.1) | copy-done | bytes 5242904
  3.1 0.0 copy-start.3
  3.1 1.1 copy-done.3
  4.3 0.0 copy-start.4
  4.3 0.7 copy-done.4
  4.9 4.8 %shard_map.113 = (bf16[1024,192]{1,0:T(8,128)(2,1)}, bf16[320,512]{1,0:T(8,128)(2,1)S(1)}, bf16[320,512]{1,0:T(8,128)(2,1)S(1)}, f32[4,1,1280]{2,1,0:T(1,128)S(1)}, f32[4,1,1280]{2,1,0:T(1,128)S(1)}) custom-call(f32[96,2048]{1,0:T(8,128)S(1)} %copy-done.3, s32[1,1024]{1,0:T(1,128)S(1)} %copy-done.4, bf16[320,16,512]{2,1,0:T(8,128)(2,1)S(1)} %copy-done.1), custom_call_target="tpu_custom_call" | custom-call | tf_op jit(solution)/shard_map/pallas_call | solution.py:79
  9.7 7.3 %all-to-all-start = ((bf16[32,32,192]{2,1,0:T(8,128)(2,1)}), bf16[32,32,192]{2,1,0:T(8,128)(2,1)S(1)}, u32[]{:S(2)}, u32[]{:S(2)}) async-start(bf16[32,32,192]{2,1,0:T(8,128)(2,1)} %bitcast.4), calls=%async_computation | async-start | bytes 1048576 | tf_op jit(solution)/shard_map/all_to_all | solution.py:401
  17.0 0.3 collective-permute-start.2
  17.3 3.3 %collective-permute-start.3 = (f32[4,1,1280]{2,1,0:T(1,128)S(1)}, f32[4,1,1280]{2,1,0:T(1,128)S(1)}, u32[]{:S(2)}, u32[]{:S(2)}) collective-permute-start(f32[4,1,1280]{2,1,0:T(1,128)S(1)} %get-tuple-element.11), channel_id=1, source_target_pairs={{0,7},{1,0},{2,1},{3,2},{4,3},{5,4},{6,5},{7,6},{8,15},{9,8},{10,9... | collective-permute-start | bytes 61448 | tf_op jit(solution)/shard_map/ppermute | solution.py:407
  20.6 1.8 %collective-permute-start = (bf16[320,512]{1,0:T(8,128)(2,1)S(1)}, bf16[320,512]{1,0:T(8,128)(2,1)S(1)}, u32[]{:S(2)}, u32[]{:S(2)}) collective-permute-start(bf16[320,512]{1,0:T(8,128)(2,1)S(1)} %get-tuple-element.8), channel_id=1, source_target_pairs={{0,8},{8,16},{16,24},{24,0},{1,9},{9,17},{17,25},{25,1},{2,10},{10... | collective-permute-start | bytes 983048 | tf_op jit(solution)/shard_map/ppermute | solution.py:404
  22.4 1.2 collective-permute-start.1
  23.5 0.0 copy-start
  23.5 2.2 %copy-done = f32[125,16,512]{2,1,0:T(8,128)S(1)} copy-done((f32[125,16,512]{2,1,0:T(8,128)S(1)}, f32[125,16,512]{2,1,0:T(8,128)}, u32[]{:S(2)}) %copy-start) | copy-done | bytes 4096024
  25.7 0.0 copy-start.2
  25.7 2.5 %copy-done.2 = bf16[320,16,512]{2,1,0:T(8,128)(2,1)S(1)} copy-done((bf16[320,16,512]{2,1,0:T(8,128)(2,1)S(1)}, bf16[320,16,512]{2,1,0:T(8,128)(2,1)}, u32[]{:S(2)}) %copy-start.2) | copy-done | bytes 5242904
  28.2 17.9 %shard_map.114.partial = f32[320,16,512]{2,1,0:T(8,128)} custom-call(f32[125,16,512]{2,1,0:T(8,128)S(1)} %copy-done, bf16[320,16,512]{2,1,0:T(8,128)(2,1)S(1)} %copy-done.2), custom_call_target="tpu_custom_call" | custom-call | flops 40000000000 | bytes 60000000 | tf_op jit(solution)/shard_map/pallas_call | solution.py:171
  46.0 0.6 add_convert_fusion.edge
  46.6 0.0 collective-permute-done.2.left
  46.6 0.0 copy-start.8
  46.7 0.0 collective-permute-done.3.right
  46.7 0.0 copy-start.9
  46.7 0.0 collective-permute-done.above
  46.7 0.0 copy-start.6
  46.7 0.0 collective-permute-done.1.below
  46.7 0.0 copy-start.7
  46.7 0.0 all-to-all-done
  46.7 0.0 copy-start.5
  46.7 0.5 copy-done.8
  47.3 0.0 copy-done.9
  47.3 0.1 copy-done.6
  47.4 0.1 copy-done.7
  47.5 0.2 copy-done.5
  47.7 74.6 %shard_map.115 = (f32[96,16,512]{2,1,0:T(8,128)}, f32[320,16,512]{2,1,0:T(8,128)}) custom-call(s32[4]{0:T(128)} %add_convert_fusion.edge, f32[32]{0:T(128)} %freq.1, bf16[1024,192]{1,0:T(8,128)(2,1)} %bitcast.6, s32[8,16,512]{2,1,0:T(8,128)} %index.1, f32[8,16,512]{2,1,0:T(8,128)} %weight.1, f32[16,512]{1,0:T(8,128)} %blend.1, f32[30,16,512]{2,1,0:T(8,128)} %gain.1, ...), custom_call_target="tpu_custom_call" | custom-call | tf_op jit(solution)/shard_map/pallas_call | solution.py:362
Async XLA Ops:
  0.6 2.5 %copy-start.1 = (bf16[320,16,512]{2,1,0:T(8,128)(2,1)S(1)}, bf16[320,16,512]{2,1,0:T(8,128)(2,1)}, u32[]{:S(2)}) copy-start(bf16[320,16,512]{2,1,0:T(8,128)(2,1)} %state.5) | copy-start | bytes 15728644
  3.1 1.1 copy-start.3
  4.3 0.7 copy-start.4
  9.7 37.0 %all-to-all-start = ((bf16[32,32,192]{2,1,0:T(8,128)(2,1)}), bf16[32,32,192]{2,1,0:T(8,128)(2,1)S(1)}, u32[]{:S(2)}, u32[]{:S(2)}) async-start(bf16[32,32,192]{2,1,0:T(8,128)(2,1)} %bitcast.4), calls=%async_computation | async-start | bytes 1048576 | tf_op jit(solution)/shard_map/all_to_all | solution.py:401
  17.0 29.6 %collective-permute-start.2 = (f32[4,1,1280]{2,1,0:T(1,128)S(1)}, f32[4,1,1280]{2,1,0:T(1,128)S(1)}, u32[]{:S(2)}, u32[]{:S(2)}) collective-permute-start(f32[4,1,1280]{2,1,0:T(1,128)S(1)} %get-tuple-element.10), channel_id=1, source_target_pairs={{0,1},{1,2},{2,3},{3,4},{4,5},{5,6},{6,7},{7,0},{8,9},{9,10},{10,1... | collective-permute-start | bytes 61448 | tf_op jit(solution)/shard_map/ppermute | solution.py:406
  17.3 29.3 %collective-permute-start.3 = (f32[4,1,1280]{2,1,0:T(1,128)S(1)}, f32[4,1,1280]{2,1,0:T(1,128)S(1)}, u32[]{:S(2)}, u32[]{:S(2)}) collective-permute-start(f32[4,1,1280]{2,1,0:T(1,128)S(1)} %get-tuple-element.11), channel_id=1, source_target_pairs={{0,7},{1,0},{2,1},{3,2},{4,3},{5,4},{6,5},{7,6},{8,15},{9,8},{10,9... | collective-permute-start | bytes 61448 | tf_op jit(solution)/shard_map/ppermute | solution.py:407
  20.6 26.1 %collective-permute-start = (bf16[320,512]{1,0:T(8,128)(2,1)S(1)}, bf16[320,512]{1,0:T(8,128)(2,1)S(1)}, u32[]{:S(2)}, u32[]{:S(2)}) collective-permute-start(bf16[320,512]{1,0:T(8,128)(2,1)S(1)} %get-tuple-element.8), channel_id=1, source_target_pairs={{0,8},{8,16},{16,24},{24,0},{1,9},{9,17},{17,25},{25,1},{2,10},{10... | collective-permute-start | bytes 983048 | tf_op jit(solution)/shard_map/ppermute | solution.py:404
  22.4 24.3 %collective-permute-start.1 = (bf16[320,512]{1,0:T(8,128)(2,1)S(1)}, bf16[320,512]{1,0:T(8,128)(2,1)S(1)}, u32[]{:S(2)}, u32[]{:S(2)}) collective-permute-start(bf16[320,512]{1,0:T(8,128)(2,1)S(1)} %get-tuple-element.9), channel_id=1, source_target_pairs={{0,24},{8,0},{16,8},{24,16},{1,25},{9,1},{17,9},{25,17},{2,26},{10... | collective-permute-start | bytes 983048 | tf_op jit(solution)/shard_map/ppermute | solution.py:405
  23.5 2.2 %copy-start = (f32[125,16,512]{2,1,0:T(8,128)S(1)}, f32[125,16,512]{2,1,0:T(8,128)}, u32[]{:S(2)}) copy-start(f32[125,16,512]{2,1,0:T(8,128)} %after.1) | copy-start | bytes 12288004
  25.7 2.5 %copy-start.2 = (bf16[320,16,512]{2,1,0:T(8,128)(2,1)S(1)}, bf16[320,16,512]{2,1,0:T(8,128)(2,1)}, u32[]{:S(2)}) copy-start(bf16[320,16,512]{2,1,0:T(8,128)(2,1)} %state.5) | copy-start | bytes 15728644
  46.6 0.6 copy-start.8
  46.7 0.6 copy-start.9
  46.7 0.7 copy-start.6
  46.7 0.8 copy-start.7
  46.7 1.0 copy-start.5

commit v2 on v0

v2 whole, which is shorter than its diff:
```python
import functools
import jax
import jax.numpy as jnp
from jax import lax
from jax.experimental import pallas as pl
from jax.experimental.pallas import tpu as pltpu
from jax.sharding import PartitionSpec as P

COMP = 3
VARS = 5
PARTS = 2
LANES = 128
SUB = 8
FIELDS = 8
F32 = jnp.float32
BF16 = jnp.bfloat16


def halves(value):
    hi = value.astype(BF16)
    lo = (value - hi.astype(F32)).astype(BF16)
    return hi, lo


def diagonal(rows, cols, offset):
    r = lax.broadcasted_iota(jnp.int32, (rows, cols), 0)
    c = lax.broadcasted_iota(jnp.int32, (rows, cols), 1)
    return jnp.where(r + offset == c, 1.0, 0.0).astype(BF16)


def faces_kernel(state, top, bottom, first, last):
    planes, rows, cols = state.shape
    r = lax.broadcasted_iota(jnp.int32, (32, 16 * rows), 0)
    c = lax.broadcasted_iota(jnp.int32, (32, 16 * rows), 1)
    want = jnp.where(r < 16, r * rows, (r - 16) * rows + rows - 1)
    ends = jnp.where(c == want, 1.0, 0.0).astype(BF16)
    for g in range(planes // 16):
        block = state[g * 16 : g * 16 + 16].reshape(16 * rows, cols)
        got = jnp.dot(ends, block, preferred_element_type=F32).astype(BF16)
        top[g * 16 : g * 16 + 16, :] = got[0:16]
        bottom[g * 16 : g * 16 + 16, :] = got[16:32]
    ec = lax.broadcasted_iota(jnp.int32, (SUB, LANES), 1)
    nt = (((1,), (1,)), ((), ()))
    pick_first = jnp.where(ec == 0, 1.0, 0.0).astype(BF16)
    pick_last = jnp.where(ec == LANES - 1, 1.0, 0.0).astype(BF16)
    left = state[:, :, 0:LANES].reshape(planes * rows, LANES)
    right = state[:, :, cols - LANES : cols].reshape(planes * rows, LANES)
    got_first = lax.dot_general(pick_first, left, nt, preferred_element_type=F32)
    got_last = lax.dot_general(pick_last, right, nt, preferred_element_type=F32)
    parts, _, length = first.shape
    for q in range(parts):
        first[q] = got_first[0:1, q * length : (q + 1) * length]
        last[q] = got_last[0:1, q * length : (q + 1) * length]


def faces(state):
    n, rows, cols = state.shape
    steps = 4
    planes = n // steps
    chunk = planes // (FIELDS * VARS)
    length = FIELDS * VARS * rows
    face = pl.BlockSpec((planes, cols), lambda g: (g, 0))
    ends = pl.BlockSpec((chunk, 1, length), lambda g: (g, 0, 0))
    return pl.pallas_call(
        faces_kernel,
        grid=(steps,),
        in_specs=[pl.BlockSpec((planes, rows, cols), lambda g: (g, 0, 0))],
        out_specs=[face, face, ends, ends],
        out_shape=[
            jax.ShapeDtypeStruct((n, cols), BF16),
            jax.ShapeDtypeStruct((n, cols), BF16),
            jax.ShapeDtypeStruct((steps * chunk, 1, length), F32),
            jax.ShapeDtypeStruct((steps * chunk, 1, length), F32),
        ],
        compiler_params=pltpu.CompilerParams(vmem_limit_bytes=60 << 20),
    )(state)


def pick_kernel(modes, nodes, after, table, split, picked):
    width, owned = modes.shape
    listed = nodes.shape[1]
    hi, lo = halves(modes[...])
    split[0:width] = hi
    split[width:] = lo
    step = min(listed, 256)
    node_rows = lax.broadcasted_iota(jnp.int32, (owned, step), 0)

    def pick(b, _):
        at = pl.ds(pl.multiple_of(b * step, step), step)
        onehot = jnp.where(node_rows == nodes[:, at], 1.0, 0.0).astype(BF16)
        picked[...] = jnp.dot(split[...], onehot, preferred_element_type=F32)
        table[at, :] = picked[...].T.astype(BF16)
        return 0

    lax.fori_loop(0, listed // step, pick, 0)


def pick_nodes(modes, nodes, after):
    width, owned = modes.shape
    listed = nodes.shape[1]
    vmem = pl.BlockSpec(memory_space=pltpu.VMEM)
    return pl.pallas_call(
        pick_kernel,
        in_specs=[vmem, vmem, pl.BlockSpec(memory_space=pl.ANY)],
        out_specs=vmem,
        out_shape=jax.ShapeDtypeStruct((listed, 2 * width), BF16),
        scratch_shapes=[
            pltpu.VMEM((2 * width, owned), BF16),
            pltpu.VMEM((2 * width, min(listed, 256)), F32),
        ],
        compiler_params=pltpu.CompilerParams(vmem_limit_bytes=60 << 20),
    )(modes, nodes, after)


def flux_kernel(edge, freq, volume, jac, state, above, below, left, right, out, coef, wide, side, halo, arrive):
    planes, rows, cols = state.shape
    blocks = cols // LANES
    high = rows // SUB
    pitch = rows + 2 * SUB
    step = pl.program_id(0)

    def fetch(b):
        return pltpu.make_async_copy(jac.at[:, :, b * LANES : b * LANES + LANES], coef.at[b], arrive.at[b])

    @pl.when(step == 0)
    def _():
        for b in range(blocks):
            fetch(b).start()
        halo[0] = above[...].astype(F32) * edge[0].astype(F32)
        halo[1] = below[...].astype(F32) * edge[1].astype(F32)

    for p in range(planes):
        here = state[p].astype(F32)
        for b in range(blocks):
            wide[b, p * pitch + SUB : p * pitch + SUB + rows, :] = here[:, b * LANES : b * LANES + LANES]
    for g in range(planes // SUB):
        at = pl.ds(pl.multiple_of(step * planes, SUB) + g * SUB, SUB)
        for b in range(blocks):
            over = slice(b * LANES, b * LANES + LANES)
            wide[b, pl.ds(g * SUB * pitch + SUB - 1, SUB, stride=pitch), :] = halo[0, at, over]
            wide[b, pl.ds(g * SUB * pitch + SUB + rows, SUB, stride=pitch), :] = halo[1, at, over]
    for which, columns in enumerate((left, right)):
        flag = edge[2 + which].astype(F32)
        for g in range(planes * rows // LANES):
            line = jnp.broadcast_to(columns[0, :, g * LANES : g * LANES + LANES] * flag, (LANES, LANES))
            side[which, g * LANES : g * LANES + LANES, :] = line.T

    lane = lax.broadcasted_iota(jnp.int32, (SUB, LANES), 1)
    for b in range(blocks):

        @pl.when(step == 0)
        def _(b=b):
            fetch(b).wait()

        def body(h, _, b=b):
            start = pl.multiple_of(h * SUB, SUB)
            at = pl.ds(start, SUB)

            def rowof(block, p, shift):
                return wide[block, pl.ds(p * pitch + SUB + shift + start, SUB), :]

            vol = volume[at, b * LANES : b * LANES + LANES]
            rates = [vol * freq[step * (FIELDS // PARTS) + c] for c in range(FIELDS // PARTS)]
            acc = [[None] * VARS for _ in range(FIELDS)]
            for u in range(VARS):
                base = [rowof(b, f * VARS + u, 0) for f in range(FIELDS)]
                for c in range(FIELDS // PARTS):
                    re, im = 2 * c, 2 * c + 1
                    for f, term in ((re, -(rates[c] * base[im])), (im, rates[c] * base[re])):
                        acc[f][u] = term if acc[f][u] is None else acc[f][u] + term
                for d in range(5):
                    q = base
                    if d == 1:
                        q = [rowof(b, f * VARS + u, -1) for f in range(FIELDS)]
                    elif d == 2:
                        q = [rowof(b, f * VARS + u, 1) for f in range(FIELDS)]
                    elif d > 2:
                        turn, fill, source = (1, LANES - 1, b - 1) if d == 3 else (LANES - 1, 0, b + 1)
                        q = []
                        for f in range(FIELDS):
                            p = f * VARS + u
                            if 0 <= source < blocks:
                                other = rowof(source, p, 0)
                            else:
                                other = side[d - 3, pl.ds(p * rows + start, SUB), :]
                            q.append(pltpu.roll(jnp.where(lane == fill, other, base[f]), turn, 1))
                    for v in range(VARS):
                        j = coef[b, d * VARS * VARS + v * VARS + u, at, :]
                        for f in range(FIELDS):
                            term = j * q[f]
                            acc[f][v] = term if acc[f][v] is None else acc[f][v] + term
            for f in range(FIELDS):
                for v in range(VARS):
                    out[f * VARS + v, at, b * LANES : b * LANES + LANES] = acc[f][v]
            return 0

        lax.fori_loop(0, high, body, 0)


def flux(edge, freq, volume, jac, state, above, below, left, right):
    n, rows, cols = state.shape
    blocks = cols // LANES
    planes = FIELDS * VARS
    scalar = pl.BlockSpec(memory_space=pltpu.SMEM)
    whole = lambda g: (0, 0)
    ends = pl.BlockSpec((1, 1, planes * rows), lambda g: (g, 0, 0))
    return pl.pallas_call(
        flux_kernel,
        grid=(n // planes,),
        in_specs=[
            scalar, scalar,
            pl.BlockSpec((rows, cols), whole),
            pl.BlockSpec(memory_space=pl.ANY),
            pl.BlockSpec((planes, rows, cols), lambda g: (g, 0, 0)),
            pl.BlockSpec((n, cols), whole), pl.BlockSpec((n, cols), whole),
            ends, ends,
        ],
        out_specs=pl.BlockSpec((planes, rows, cols), lambda g: (g, 0, 0)),
        out_shape=jax.ShapeDtypeStruct((n, rows, cols), F32),
        scratch_shapes=[
            pltpu.VMEM((blocks, jac.shape[0], rows, LANES), F32),
            pltpu.VMEM((blocks, planes * (rows + 2 * SUB), LANES), F32),
            pltpu.VMEM((2, planes * rows, LANES), F32),
            pltpu.VMEM((2, n, cols), F32),
            pltpu.SemaphoreType.DMA((blocks,)),
        ],
        compiler_params=pltpu.CompilerParams(vmem_limit_bytes=60 << 20),
        cost_estimate=pl.CostEstimate(flops=40_000_000_000, bytes_accessed=60_000_000, transcendentals=0),
    )(edge, freq, volume, jac, state, above, below, left, right)


SEG = 32
RANKS = 2
SPARE = 2


def finish_kernel(
    freq, table, index, weight, blend, gain, partial, motion, residual,
    modes, lists_e, lists_w, spare_e, spare_w, moved, even,
):
    slots, width2 = table.shape
    width = width2 // 2
    entries = index.shape[0]
    cases = width // COMP
    owners = slots // SEG

    @pl.when((pl.program_id(0) == 0) & (pl.program_id(1) == 0))
    def _():
        step = min(slots, 512)
        for b in range(slots // step):
            turned = table[b * step : b * step + step, :].astype(F32).T.astype(BF16)
            modes[:, b * step : b * step + step] = turned
            modes[0:width, slots + b * step : slots + b * step + step] = turned[0:width]
            modes[width:, slots + b * step : slots + b * step + step] = jnp.zeros((width, step), BF16)

    raw = [jnp.where(index[k] >= 0, weight[k], 0.0) for k in range(entries)]
    total = raw[0]
    for k in range(1, entries):
        total = total + raw[k]
    scale = blend[...] / total
    share = [r * scale for r in raw]
    key = [index[k] for k in range(entries)]
    for k in range(entries):
        for m in range(k + 1, entries):
            same = key[k] == key[m]
            share[k] = jnp.where(same, share[k] + share[m], share[k])
            key[m] = jnp.where(same, -1, key[m])
    owner = [jnp.where(e < 0, -1 - k, e // SEG) for k, e in enumerate(key)]
    zero = jnp.zeros(owner[0].shape, jnp.int32)
    spare = []
    listed = []
    count = zero
    for k in range(entries):
        rank = zero
        for m in range(k):
            rank = rank + jnp.where(owner[m] == owner[k], 1, 0)
        over = (rank >= RANKS) & (key[k] >= 0)
        spare.append(jnp.where(over, count, -1))
        count = count + jnp.where(over, 1, 0)
        listed.append(jnp.where(over | (key[k] < 0), -1, owner[k] + rank * owners))
    for o in range(entries - RANKS):
        e = zero - 1
        w = jnp.zeros(zero.shape, F32)
        for k in range(entries):
            hit = spare[k] == o
            e = jnp.where(hit, key[k], e)
            w = jnp.where(hit, share[k], w)
        spare_e[o] = e
        spare_w[o] = w

    local = [e % SEG for e in key]

    def fill(i, _):
        e = zero - 1
        w = jnp.zeros(zero.shape, F32)
        for k in range(entries):
            hit = listed[k] == i
            e = jnp.where(hit, local[k], e)
            w = jnp.where(hit, share[k], w)
        lists_e[i] = e
        lists_w[i] = w
        return 0

    lax.fori_loop(0, owners * RANKS, fill, 0, unroll=4)

    slot_rows = lax.broadcasted_iota(jnp.int32, (SUB, LANES), 0)
    places = [slot_rows + q * SUB for q in range(SEG // SUB)]

    def spread(ref, i, row):
        return jnp.broadcast_to(ref[i, pl.ds(row, 1), :], (SUB, LANES))

    def put(into, s, part, pairs):
        got = []
        for ids in places:
            value = 0.0
            for e, w in pairs:
                value = jnp.where(ids == e, w, value)
            got.append(value)
        high, low = halves(jnp.concatenate(got, axis=0))
        at = pl.multiple_of(s * SEG, SEG)
        into[pl.ds(at, SEG), part * LANES : part * LANES + LANES] = high
        into[pl.ds(at + slots, SEG), part * LANES : part * LANES + LANES] = low

    def product(source):
        got = jnp.dot(modes[...], source[...], preferred_element_type=F32)
        return got[0:width] + got[width:]

    def place(sums, pair, add=False):
        for part in range(2):
            for c in range(width // SUB):
                at = pl.ds(c * SUB * SUB + pair * 2 + part, SUB, stride=SUB)
                value = sums[c * SUB : c * SUB + SUB, part * LANES : part * LANES + LANES]
                moved[at, :] = moved[at, :] + value if add else value

    chunk = min(slots, 256)

    def tile(pair, first, extra):
        highs, lows = [], []
        for q in range(chunk // SEG):
            s = first + q
            sides = []
            for part in range(2):
                row = pair * 2 + part
                pairs = [(spread(lists_e, s + r * owners, row), spread(lists_w, s + r * owners, row)) for r in range(RANKS)]
                pairs += [(e - s * SEG, w) for e, w in extra[part]]
                got = []
                for ids in places:
                    value = 0.0
                    for e, w in pairs:
                        value = jnp.where(ids == e, w, value)
                    got.append(value)
                sides.append(halves(jnp.concatenate(got, axis=0)))
            highs.append(jnp.concatenate([sides[0][0], sides[1][0]], axis=1))
            lows.append(jnp.concatenate([sides[0][1], sides[1][1]], axis=1))
        return jnp.concatenate(highs, axis=0), jnp.concatenate(lows, axis=0)

    def one_pair(pair):
        extra = [[(spread(spare_e, o, pair * 2 + part), spread(spare_w, o, pair * 2 + part)) for o in range(SPARE)] for part in range(2)]
        both = rest = None
        for c in range(slots // chunk):
            high, low = tile(pair, c * (chunk // SEG), extra)
            at = slice(c * chunk, c * chunk + chunk)
            x = jnp.dot(modes[:, at], high, preferred_element_type=F32)
            y = jnp.dot(modes[0:width, at], low, preferred_element_type=F32)
            both = x if both is None else both + x
            rest = y if rest is None else rest + y
        place(both[0:width] + both[width:] + rest, pair)

    def step_pair(pair, _):
        one_pair(pair)
        return 0

    lax.fori_loop(0, SUB // 2, step_pair, 0)

    most = jnp.max(count)

    @pl.when(most > SPARE)
    def _():
        def again(o, _):
            def one(pair, _):
                for part in range(2):
                    row = pair * 2 + part
                    e, w = spread(spare_e, o, row), spread(spare_w, o, row)

                    def rebuild(s, _):
                        put(even, s, part, [(e - s * SEG, w)])
                        return 0

                    lax.fori_loop(0, owners, rebuild, 0)
                place(product(even), pair, True)
                return 0

            lax.fori_loop(0, SUB // 2, one, 0)
            return 0

        lax.fori_loop(SPARE, most, again, 0)

    gains = [gain[i] for i in range(2 * VARS * COMP)]

    def force(c, _):
        omega = freq[c]
        m = [moved[pl.ds(pl.multiple_of((c * COMP + x) * SUB, SUB), SUB), :] for x in range(COMP)]
        for x in range(COMP):
            motion[c * COMP + x] = m[x]
        for v in range(VARS):
            pos = gains[v * COMP] * m[0]
            vel = gains[(VARS + v) * COMP] * m[0]
            for x in range(1, COMP):
                pos = pos + gains[v * COMP + x] * m[x]
                vel = vel + gains[(VARS + v) * COMP + x] * m[x]
            at = c * PARTS * VARS + v
            residual[at] = partial[at] + pos
            residual[at + VARS] = partial[at + VARS] + omega * vel
        return 0

    lax.fori_loop(0, cases, force, 0, unroll=2)


def finish(freq, table, index, weight, blend, gain, partial):
    n, rows, cols = partial.shape
    slots, width2 = table.shape
    width = width2 // 2
    entries = index.shape[0]
    owners = slots // SEG
    cells = lambda lead: pl.BlockSpec((lead, SUB, LANES), lambda b, h: (0, h, b))
    flat = pl.BlockSpec((SUB, LANES), lambda b, h: (h, b))
    return pl.pallas_call(
        finish_kernel,
        grid=(cols // LANES, rows // SUB),
        in_specs=[
            pl.BlockSpec(memory_space=pltpu.SMEM),
            pl.BlockSpec(table.shape, lambda b, h: (0, 0)),
            cells(entries), cells(entries), flat, cells(gain.shape[0]), cells(n),
        ],
        out_specs=[cells(width), cells(n)],
        out_shape=[
            jax.ShapeDtypeStruct((width, rows, cols), F32),
            jax.ShapeDtypeStruct((n, rows, cols), F32),
        ],
        scratch_shapes=[
            pltpu.VMEM((width2, 2 * slots), BF16),
            pltpu.VMEM((owners * RANKS, SUB, LANES), jnp.int32),
            pltpu.VMEM((owners * RANKS, SUB, LANES), F32),
            pltpu.VMEM((entries - RANKS, SUB, LANES), jnp.int32),
            pltpu.VMEM((entries - RANKS, SUB, LANES), F32),
            pltpu.VMEM((width * SUB, LANES), F32),
            pltpu.VMEM((2 * slots, 2 * LANES), BF16),
        ],
        compiler_params=pltpu.CompilerParams(vmem_limit_bytes=60 << 20),
    )(freq, table, index, weight, blend, gain, partial)


def ring(axis, step):
    peers = lax.axis_size(axis)
    return [(i, (i + step) % peers) for i in range(peers)]


def local(mode_shapes, send_nodes, interp_index, interp_weight, blend, motion_gain, frequency, volume, jacobian, state):
    axes = ("group", "dom")
    top, bottom, first, last = faces(state)
    table = pick_nodes(mode_shapes, send_nodes, first)
    peers = lax.axis_size(axes)
    listed, width2 = table.shape
    above = lax.ppermute(bottom, "group", ring("group", 1))
    below = lax.ppermute(top, "group", ring("group", -1))
    left = lax.ppermute(last, "dom", ring("dom", 1))
    right = lax.ppermute(first, "dom", ring("dom", -1))
    arrived = lax.all_to_all(
        table.reshape(peers, listed // peers, width2), axes, split_axis=0, concat_axis=0, tiled=True
    ).reshape(listed, width2)
    gi, gn = lax.axis_index("group"), lax.axis_size("group")
    di, dn = lax.axis_index("dom"), lax.axis_size("dom")
    edge = jnp.stack([gi > 0, gi < gn - 1, di > 0, di < dn - 1]).astype(jnp.int32)
    partial = flux(edge, frequency, volume, jacobian, state, above, below, left, right)
    return tuple(finish(frequency, arrived, interp_index, interp_weight, blend, motion_gain, partial))


def solution(mesh):
    both = ("group", "dom")
    cells3 = P(None, "group", "dom")
    cells2 = P("group", "dom")
    placed = (P(None, both), P(both, None), cells3, cells3, cells2, cells3, P(), cells2, cells3, cells3)
    return jax.shard_map(local, mesh=mesh, in_specs=placed, out_specs=(cells3, cells3), check_vma=False)
```

time: 370 us -> 90.4 us (0.24)
  the two profiles are of different devices: /device:TPU:0 before, /device:TPU:24 now
where the time goes in v2:
time: 90.4 us; the launch traced here: 91.7 us
  Pallas kernels  72.8 us (81%)
  starting transfers between devices  9.64 us (11%)
  waiting for transfers between devices  6.44 us (7%)
  local copies, waits for them, and re-layouts  1.53 us (2%)
    pallas_call x1, Pallas kernels, finish(): pl.pallas_call(finish_kernel, grid=(cols // LANES, rows // SUB), in_specs...  34.2 us
    pallas_call x1, Pallas kernels, flux(): pl.pallas_call(flux_kernel, grid=(n // planes,), in_specs=[scalar, scalar...  29.6 us
    ppermute x1, waiting for transfers between devices, local(): below = lax.ppermute(top, 'group', ring('group', -1))  6.43 us
    all_to_all x1, starting transfers between devices, local(): lax.all_to_all(table.reshape(peers, listed // peers, width2), axes, split...  4.97 us
    pallas_call x1, Pallas kernels, faces(): pl.pallas_call(faces_kernel, grid=(steps,), in_specs=[pl.BlockSpec((plane...  4.97 us
    pallas_call x1, Pallas kernels, pick_nodes(): pl.pallas_call(pick_kernel, in_specs=[vmem, vmem, pl.BlockSpec(memory_spa...  4 us
  transfers between devices with their start and end apart: 5, of which 1 were waited for; matrix products, arithmetic and copies ran while one was open for 1% of the time, Pallas kernels for 37%

profile of v2, /device:TPU:24, one launch (start us, length us, event | category | flops | bytes accessed | tf_op | source)
XLA Modules:
  0.0 91.7 jit_solution(13368210908276093432)
XLA Ops:
  0.6 5.0 %shard_map.113 = (bf16[320,512]{1,0:T(8,128)(2,1)}, bf16[320,512]{1,0:T(8,128)(2,1)}, f32[8,1,640]{2,1,0:T(1,128)}, f32[8,1,640]{2,1,0:T(1,128)}) custom-call(bf16[320,16,512]{2,1,0:T(8,128)(2,1)} %state.3), custom_call_target="tpu_custom_call" | custom-call | tf_op jit(solution)/shard_map/pallas_call | solution.py:64
  5.6 1.5 %collective-permute-start = (bf16[320,512]{1,0:T(8,128)(2,1)}, bf16[320,512]{1,0:T(8,128)(2,1)S(1)}, u32[]{:S(2)}, u32[]{:S(2)}) collective-permute-start(bf16[320,512]{1,0:T(8,128)(2,1)} %get-tuple-element.7), channel_id=1, source_target_pairs={{0,8},{8,16},{16,24},{24,0},{1,9},{9,17},{17,25},{25,1},{2,10},{10... | collective-permute-start | bytes 983048 | tf_op jit(solution)/shard_map/ppermute | solution.py:464
  7.1 1.4 %collective-permute-start.1 = (bf16[320,512]{1,0:T(8,128)(2,1)}, bf16[320,512]{1,0:T(8,128)(2,1)S(1)}, u32[]{:S(2)}, u32[]{:S(2)}) collective-permute-start(bf16[320,512]{1,0:T(8,128)(2,1)} %get-tuple-element.8), channel_id=1, source_target_pairs={{0,24},{8,0},{16,8},{24,16},{1,25},{9,1},{17,9},{25,17},{2,26},{10... | collective-permute-start | bytes 983048 | tf_op jit(solution)/shard_map/ppermute | solution.py:465
  8.5 0.0 collective-permute-start.2
  8.5 1.7 %collective-permute-start.3 = (f32[8,1,640]{2,1,0:T(1,128)}, f32[8,1,640]{2,1,0:T(1,128)S(1)}, u32[]{:S(2)}, u32[]{:S(2)}) collective-permute-start(f32[8,1,640]{2,1,0:T(1,128)} %get-tuple-element.6.after), channel_id=1, source_target_pairs={{0,7},{1,0},{2,1},{3,2},{4,3},{5,4},{6,5},{7,6},{8,15},{9,8},{10,9... | collective-permute-start | bytes 61448 | tf_op jit(solution)/shard_map/ppermute | solution.py:467
  10.3 4.0 %shard_map.114 = bf16[1024,192]{1,0:T(8,128)(2,1)} custom-call(f32[96,2048]{1,0:T(8,128)} %modes.1, s32[1,1024]{1,0:T(1,128)} %nodes.1, f32[8,1,640]{2,1,0:T(1,128)} %get-tuple-element.6.after), custom_call_target="tpu_custom_call" | custom-call | tf_op jit(solution)/shard_map/pallas_call | solution.py:102
  14.3 5.0 %all-to-all-start = ((bf16[32,32,192]{2,1,0:T(8,128)(2,1)}), bf16[32,32,192]{2,1,0:T(8,128)(2,1)S(1)}, u32[]{:S(2)}, u32[]{:S(2)}) async-start(bf16[32,32,192]{2,1,0:T(8,128)(2,1)} %bitcast.7), calls=%async_computation | async-start | bytes 1048576 | tf_op jit(solution)/shard_map/all_to_all | solution.py:468
  19.3 0.6 add_convert_fusion.edge
  19.9 0.0 collective-permute-done.2.left
  19.9 0.0 copy-start.3
  19.9 0.0 collective-permute-done.3.right
  19.9 0.0 copy-start.4
  19.9 0.0 collective-permute-done.above
  19.9 0.0 copy-start.1
  19.9 6.4 %collective-permute-done.1.below = bf16[320,512]{1,0:T(8,128)(2,1)S(1)} collective-permute-done((bf16[320,512]{1,0:T(8,128)(2,1)}, bf16[320,512]{1,0:T(8,128)(2,1)S(1)}, u32[]{:S(2)}, u32[]{:S(2)}) %collective-permute-start.1) | collective-permute-done | bytes 327712 | tf_op jit(solution)/shard_map/ppermute | solution.py:465
  26.3 0.0 copy-done.3
  26.3 0.0 copy-done.4
  26.3 0.0 copy-done.1
  26.3 0.0 copy-start.2
  26.4 0.7 copy-done.2
  27.1 29.6 %shard_map.115.partial = f32[320,16,512]{2,1,0:T(8,128)} custom-call(s32[4]{0:T(128)} %add_convert_fusion.edge, f32[32]{0:T(128)} %freq.3, f32[16,512]{1,0:T(8,128)} %volume.1, f32[125,16,512]{2,1,0:T(8,128)} %jac.1, bf16[320,16,512]{2,1,0:T(8,128)(2,1)} %state.3, bf16[320,512]{1,0:T(8,128)(2,1)} %copy-done.1, bf16[320,512]{1,0:T(8,128)(2,1)} %copy-done.2, ...), custom_call_target="tpu_custom_call" | custom-call | flops 40000000000 | bytes 60000000 | tf_op jit(solution)/shard_map/pallas_call | solution.py:207
  56.6 0.0 all-to-all-done
  56.6 0.0 copy-start
  56.6 0.8 copy-done
  57.4 34.2 %shard_map.116 = (f32[96,16,512]{2,1,0:T(8,128)}, f32[320,16,512]{2,1,0:T(8,128)}) custom-call(f32[32]{0:T(128)} %freq.3, bf16[1024,192]{1,0:T(8,128)(2,1)} %bitcast.6, s32[8,16,512]{2,1,0:T(8,128)} %index.1, f32[8,16,512]{2,1,0:T(8,128)} %weight.1, f32[16,512]{1,0:T(8,128)} %blend.1, f32[30,16,512]{2,1,0:T(8,128)} %gain.1, f32[320,16,512]{2,1,0:T(8,128)} %shard_map.115.partial), custom_call_target="tpu_custom_call" | custom-call | tf_op jit(solution)/shard_map/pallas_call | solution.py:427
Async XLA Ops:
  5.6 14.3 %collective-permute-start = (bf16[320,512]{1,0:T(8,128)(2,1)}, bf16[320,512]{1,0:T(8,128)(2,1)S(1)}, u32[]{:S(2)}, u32[]{:S(2)}) collective-permute-start(bf16[320,512]{1,0:T(8,128)(2,1)} %get-tuple-element.7), channel_id=1, source_target_pairs={{0,8},{8,16},{16,24},{24,0},{1,9},{9,17},{17,25},{25,1},{2,10},{10... | collective-permute-start | bytes 983048 | tf_op jit(solution)/shard_map/ppermute | solution.py:464
  7.1 19.2 %collective-permute-start.1 = (bf16[320,512]{1,0:T(8,128)(2,1)}, bf16[320,512]{1,0:T(8,128)(2,1)S(1)}, u32[]{:S(2)}, u32[]{:S(2)}) collective-permute-start(bf16[320,512]{1,0:T(8,128)(2,1)} %get-tuple-element.8), channel_id=1, source_target_pairs={{0,24},{8,0},{16,8},{24,16},{1,25},{9,1},{17,9},{25,17},{2,26},{10... | collective-permute-start | bytes 983048 | tf_op jit(solution)/shard_map/ppermute | solution.py:465
  8.5 11.3 %collective-permute-start.2 = (f32[8,1,640]{2,1,0:T(1,128)}, f32[8,1,640]{2,1,0:T(1,128)S(1)}, u32[]{:S(2)}, u32[]{:S(2)}) collective-permute-start(f32[8,1,640]{2,1,0:T(1,128)} %get-tuple-element.9), channel_id=1, source_target_pairs={{0,1},{1,2},{2,3},{3,4},{4,5},{5,6},{6,7},{7,0},{8,9},{9,10},{10,1... | collective-permute-start | bytes 61448 | tf_op jit(solution)/shard_map/ppermute | solution.py:466
  8.5 11.3 %collective-permute-start.3 = (f32[8,1,640]{2,1,0:T(1,128)}, f32[8,1,640]{2,1,0:T(1,128)S(1)}, u32[]{:S(2)}, u32[]{:S(2)}) collective-permute-start(f32[8,1,640]{2,1,0:T(1,128)} %get-tuple-element.6.after), channel_id=1, source_target_pairs={{0,7},{1,0},{2,1},{3,2},{4,3},{5,4},{6,5},{7,6},{8,15},{9,8},{10,9... | collective-permute-start | bytes 61448 | tf_op jit(solution)/shard_map/ppermute | solution.py:467
  14.3 42.4 %all-to-all-start = ((bf16[32,32,192]{2,1,0:T(8,128)(2,1)}), bf16[32,32,192]{2,1,0:T(8,128)(2,1)S(1)}, u32[]{:S(2)}, u32[]{:S(2)}) async-start(bf16[32,32,192]{2,1,0:T(8,128)(2,1)} %bitcast.7), calls=%async_computation | async-start | bytes 1048576 | tf_op jit(solution)/shard_map/all_to_all | solution.py:468
  19.9 6.5 %copy-start.3 = (f32[8,1,640]{2,1,0:T(1,128)}, f32[8,1,640]{2,1,0:T(1,128)S(1)}, u32[]{:S(2)}) copy-start(f32[8,1,640]{2,1,0:T(1,128)S(1)} %collective-permute-done.2.left) | copy-start | bytes 61444
  19.9 6.5 %copy-start.4 = (f32[8,1,640]{2,1,0:T(1,128)}, f32[8,1,640]{2,1,0:T(1,128)S(1)}, u32[]{:S(2)}) copy-start(f32[8,1,640]{2,1,0:T(1,128)S(1)} %collective-permute-done.3.right) | copy-start | bytes 61444
  19.9 6.4 %copy-start.1 = (bf16[320,512]{1,0:T(8,128)(2,1)}, bf16[320,512]{1,0:T(8,128)(2,1)S(1)}, u32[]{:S(2)}) copy-start(bf16[320,512]{1,0:T(8,128)(2,1)S(1)} %collective-permute-done.above) | copy-start | bytes 983044
  26.3 0.7 copy-start.2
  56.6 0.8 copy-start

commit v3 on v2

v3 whole, which is shorter than its diff:
```python
import functools
import jax
import jax.numpy as jnp
from jax import lax
from jax.experimental import pallas as pl
from jax.experimental.pallas import tpu as pltpu
from jax.sharding import PartitionSpec as P

COMP = 3
VARS = 5
PARTS = 2
LANES = 128
SUB = 8
FIELDS = 8
ORDER = (0, 3, 1, 4, 2)
F32 = jnp.float32
BF16 = jnp.bfloat16


def halves(value):
    hi = value.astype(BF16)
    lo = (value - hi.astype(F32)).astype(BF16)
    return hi, lo


def faces_kernel(source, top, bottom, first, last, state, plain, arrive):
    count, planes, rows, cols = state.shape
    copies = [
        pltpu.make_async_copy(source.at[s * planes : (s + 1) * planes], state.at[s], arrive.at[s]) for s in range(count)
    ]
    for copy in copies:
        copy.start()
    for s, copy in enumerate(copies):
        copy.wait()
        cut_faces(s, state.at[s], top, bottom, first, last, plain)


def cut_faces(step, state, top, bottom, first, last, plain):
    planes, rows, cols = state.shape
    group = 16
    for g in range(planes // group):
        for p in range(group):
            here = state[g * group + p].astype(F32)
            for b in range(cols // LANES):
                plain[b, p * rows : p * rows + rows, :] = here[:, b * LANES : b * LANES + LANES]
        at = slice(step * planes + g * group, step * planes + g * group + group)
        for b in range(cols // LANES):
            over = slice(b * LANES, b * LANES + LANES)
            for ref, row in ((top, 0), (bottom, rows - 1)):
                ref[at, over] = jnp.concatenate(
                    [plain[b, pl.ds(half * SUB * rows + row, SUB, stride=rows), :] for half in range(group // SUB)], axis=0
                ).astype(BF16)
    r = lax.broadcasted_iota(jnp.int32, (SUB, 2 * LANES), 0)
    c = lax.broadcasted_iota(jnp.int32, (SUB, 2 * LANES), 1)
    pick = jnp.where(c == r * (2 * LANES - 1), 1.0, 0.0).astype(BF16)
    nt = (((1,), (1,)), ((), ()))
    sides = jnp.concatenate([state[:, :, 0:LANES], state[:, :, cols - LANES : cols]], axis=2)
    got = lax.dot_general(pick, sides.reshape(planes * rows, 2 * LANES), nt, preferred_element_type=F32)
    _, _, length = first.shape
    parts = planes * rows // length
    for q in range(parts):
        first[step * parts + q] = got[0:1, q * length : (q + 1) * length]
        last[step * parts + q] = got[1:2, q * length : (q + 1) * length]


def faces(state):
    n, rows, cols = state.shape
    steps = 4
    planes = n // steps
    chunk = planes // (FIELDS * VARS)
    length = FIELDS * VARS * rows
    vmem = pl.BlockSpec(memory_space=pltpu.VMEM)
    return pl.pallas_call(
        faces_kernel,
        in_specs=[pl.BlockSpec(memory_space=pl.ANY)],
        out_specs=[vmem] * 4,
        out_shape=[
            jax.ShapeDtypeStruct((n, cols), BF16),
            jax.ShapeDtypeStruct((n, cols), BF16),
            jax.ShapeDtypeStruct((steps * chunk, 1, length), F32),
            jax.ShapeDtypeStruct((steps * chunk, 1, length), F32),
        ],
        scratch_shapes=[
            pltpu.VMEM((steps, planes, rows, cols), BF16),
            pltpu.VMEM((cols // LANES, 16 * rows, LANES), F32),
            pltpu.SemaphoreType.DMA((steps,)),
        ],
        compiler_params=pltpu.CompilerParams(vmem_limit_bytes=63 << 20),
    )(state)


def pick_kernel(modes, nodes, after, table, split):
    width, owned = modes.shape
    listed = nodes.shape[1]
    hi, lo = halves(modes[...])
    split[0:width] = hi
    split[width:] = lo
    step = min(listed, 256)
    deep = min(owned, 256)
    node_rows = lax.broadcasted_iota(jnp.int32, (deep, step), 0)

    def pick(b, _):
        at = pl.ds(pl.multiple_of(b * step, step), step)
        wanted = jnp.broadcast_to(nodes[:, at], (deep, step))
        total = None
        for k in range(owned // deep):
            onehot = jnp.where(node_rows == wanted - k * deep, 1.0, 0.0).astype(BF16)
            part = jnp.dot(split[:, k * deep : k * deep + deep], onehot, preferred_element_type=F32)
            total = part if total is None else total + part
        table[at, :] = total.T.astype(BF16)
        return 0

    lax.fori_loop(0, listed // step, pick, 0)


def pick_nodes(modes, nodes, after):
    width, owned = modes.shape
    listed = nodes.shape[1]
    vmem = pl.BlockSpec(memory_space=pltpu.VMEM)
    return pl.pallas_call(
        pick_kernel,
        in_specs=[vmem, vmem, pl.BlockSpec(memory_space=pl.ANY)],
        out_specs=vmem,
        out_shape=jax.ShapeDtypeStruct((listed, 2 * width), BF16),
        scratch_shapes=[pltpu.VMEM((2 * width, owned), BF16)],
        compiler_params=pltpu.CompilerParams(vmem_limit_bytes=63 << 20),
    )(modes, nodes, after)


def flux_kernel(flags, freq, volume, jac, state, above, below, left, right, out, coef, wide, side, halo, arrive):
    planes, rows, cols = state.shape
    blocks = cols // LANES
    high = rows // SUB
    pitch = rows + 2 * SUB
    step = pl.program_id(0)
    place = [lax.axis_index(axis) for axis in ("group", "dom")]
    edge = [part for i, n in zip(place, flags) for part in (i > 0, i < n - 1)]

    def fetch(b):
        return pltpu.make_async_copy(jac.at[:, :, b * LANES : b * LANES + LANES], coef.at[b], arrive.at[b])

    @pl.when(step == 0)
    def _():
        for b in range(blocks):
            fetch(b).start()
        halo[0] = above[...].astype(F32) * jnp.where(edge[0], 1.0, 0.0)
        halo[1] = below[...].astype(F32) * jnp.where(edge[1], 1.0, 0.0)

    for p in range(planes):
        here = state[p].astype(F32)
        for b in range(blocks):
            wide[b, p * pitch + SUB : p * pitch + SUB + rows, :] = here[:, b * LANES : b * LANES + LANES]
    for g in range(planes // SUB):
        at = pl.ds(pl.multiple_of(step * planes, SUB) + g * SUB, SUB)
        for b in range(blocks):
            over = slice(b * LANES, b * LANES + LANES)
            wide[b, pl.ds(g * SUB * pitch + SUB - 1, SUB, stride=pitch), :] = halo[0, at, over]
            wide[b, pl.ds(g * SUB * pitch + SUB + rows, SUB, stride=pitch), :] = halo[1, at, over]
    for which, columns in enumerate((left, right)):
        flag = jnp.where(edge[2 + which], 1.0, 0.0)
        for g in range(planes * rows // LANES):
            line = jnp.broadcast_to(columns[0, :, g * LANES : g * LANES + LANES] * flag, (LANES, LANES))
            side[which, g * LANES : g * LANES + LANES, :] = line.T

    lane = lax.broadcasted_iota(jnp.int32, (SUB, LANES), 1)
    for b in range(blocks):

        @pl.when(step == 0)
        def _(b=b):
            fetch(b).wait()

        def body(h, _, b=b):
            start = pl.multiple_of(h * SUB, SUB)
            at = pl.ds(start, SUB)

            def rowof(block, p, shift):
                return wide[block, pl.ds(p * pitch + SUB + shift + start, SUB), :]

            vol = volume[at, b * LANES : b * LANES + LANES]
            rates = [vol * freq[step * (FIELDS // PARTS) + c] for c in range(FIELDS // PARTS)]
            acc = [[None] * VARS for _ in range(FIELDS)]

            def operand(u, d):
                centre = [rowof(b, f * VARS + u, 0) for f in range(FIELDS)] if d != 1 and d != 2 else None
                if d == 0:
                    return centre
                if d == 1:
                    return [rowof(b, f * VARS + u, -1) for f in range(FIELDS)]
                if d == 2:
                    return [rowof(b, f * VARS + u, 1) for f in range(FIELDS)]
                turn, fill, source = (1, LANES - 1, b - 1) if d == 3 else (LANES - 1, 0, b + 1)
                q = []
                for f in range(FIELDS):
                    p = f * VARS + u
                    if 0 <= source < blocks:
                        other = rowof(source, p, 0)
                    else:
                        other = side[d - 3, pl.ds(p * rows + start, SUB), :]
                    q.append(pltpu.roll(jnp.where(lane == fill, other, centre[f]), turn, 1))
                return q

            stages = [(u, d) for u in range(VARS) for d in ORDER]
            ahead = operand(*stages[0])
            for n, (u, d) in enumerate(stages):
                q = ahead
                if n + 1 < len(stages):
                    ahead = operand(*stages[n + 1])
                if d == 0:
                    for c in range(FIELDS // PARTS):
                        re, im = 2 * c, 2 * c + 1
                        for f, term in ((re, -(rates[c] * q[im])), (im, rates[c] * q[re])):
                            acc[f][u] = term if acc[f][u] is None else acc[f][u] + term
                for v in range(VARS):
                    j = coef[b, d * VARS * VARS + v * VARS + u, at, :]
                    for f in range(FIELDS):
                        term = j * q[f]
                        acc[f][v] = term if acc[f][v] is None else acc[f][v] + term
            for f in range(FIELDS):
                for v in range(VARS):
                    out[f * VARS + v, at, b * LANES : b * LANES + LANES] = acc[f][v]
            return 0

        lax.fori_loop(0, high, body, 0)


def flux(freq, volume, jac, state, above, below, left, right):
    n, rows, cols = state.shape
    blocks = cols // LANES
    planes = FIELDS * VARS
    scalar = pl.BlockSpec(memory_space=pltpu.SMEM)
    whole = lambda g: (0, 0)
    ends = pl.BlockSpec((1, 1, planes * rows), lambda g: (g, 0, 0))
    return pl.pallas_call(
        functools.partial(flux_kernel, [lax.axis_size(axis) for axis in ("group", "dom")]),
        grid=(n // planes,),
        in_specs=[
            scalar,
            pl.BlockSpec((rows, cols), whole),
            pl.BlockSpec(memory_space=pl.ANY),
            pl.BlockSpec((planes, rows, cols), lambda g: (g, 0, 0)),
            pl.BlockSpec((n, cols), whole), pl.BlockSpec((n, cols), whole),
            ends, ends,
        ],
        out_specs=pl.BlockSpec((planes, rows, cols), lambda g: (g, 0, 0)),
        out_shape=jax.ShapeDtypeStruct((n, rows, cols), F32),
        scratch_shapes=[
            pltpu.VMEM((blocks, jac.shape[0], rows, LANES), F32),
            pltpu.VMEM((blocks, planes * (rows + 2 * SUB), LANES), F32),
            pltpu.VMEM((2, planes * rows, LANES), F32),
            pltpu.VMEM((2, n, cols), F32),
            pltpu.SemaphoreType.DMA((blocks,)),
        ],
        compiler_params=pltpu.CompilerParams(vmem_limit_bytes=63 << 20),
        cost_estimate=pl.CostEstimate(flops=40_000_000_000, bytes_accessed=60_000_000, transcendentals=0),
    )(freq, volume, jac, state, above, below, left, right)


SHIFT = 5
SEG = 1 << SHIFT
RANKS = 2
SPARE = 2


def lists_kernel(index, weight, blend, lists_e, lists_w, spare_e, spare_w, counts):
    entries = index.shape[0]
    owners = lists_e.shape[0] // RANKS

    raw = [jnp.where(index[k] >= 0, weight[k], 0.0) for k in range(entries)]
    total = raw[0]
    for k in range(1, entries):
        total = total + raw[k]
    scale = blend[...] / total
    share = [r * scale for r in raw]
    key = [index[k] for k in range(entries)]
    for k in range(entries):
        for m in range(k + 1, entries):
            same = key[k] == key[m]
            share[k] = jnp.where(same, share[k] + share[m], share[k])
            key[m] = jnp.where(same, -1, key[m])
    owner = [jnp.where(e < 0, -1 - k, e >> SHIFT) for k, e in enumerate(key)]
    zero = jnp.zeros(owner[0].shape, jnp.int32)
    spare = []
    listed = []
    count = zero
    for k in range(entries):
        rank = zero
        for m in range(k):
            rank = rank + jnp.where(owner[m] == owner[k], 1, 0)
        over = (rank >= RANKS) & (key[k] >= 0)
        spare.append(jnp.where(over, count, -1))
        count = count + jnp.where(over, 1, 0)
        listed.append(jnp.where(over | (key[k] < 0), -1, owner[k] + rank * owners))
    for o in range(entries - RANKS):
        e = zero - 1
        w = jnp.zeros(zero.shape, F32)
        for k in range(entries):
            hit = spare[k] == o
            e = jnp.where(hit, key[k], e)
            w = jnp.where(hit, share[k], w)
        spare_e[o] = e
        spare_w[o] = w

    local = [e & (SEG - 1) for e in key]

    def fill(i, _):
        e = zero - 1
        w = jnp.zeros(zero.shape, F32)
        for k in range(entries):
            hit = listed[k] == i
            e = jnp.where(hit, local[k], e)
            w = jnp.where(hit, share[k], w)
        lists_e[i] = e
        lists_w[i] = w
        return 0

    lax.fori_loop(0, owners * RANKS, fill, 0, unroll=4)
    counts[...] = count


def owner_lists(index, weight, blend, slots):
    entries, rows, cols = index.shape
    owners = slots // SEG
    cells = lambda lead: pl.BlockSpec((lead, rows, LANES), lambda b: (0, 0, b))
    flat = pl.BlockSpec((rows, LANES), lambda b: (0, b))
    made = [
        (owners * RANKS, jnp.int32), (owners * RANKS, F32), (entries - RANKS, jnp.int32), (entries - RANKS, F32),
    ]
    return pl.pallas_call(
        lists_kernel,
        grid=(cols // LANES,),
        in_specs=[cells(entries), cells(entries), flat],
        out_specs=[cells(lead) for lead, _ in made] + [flat],
        out_shape=[jax.ShapeDtypeStruct((lead, rows, cols), kind) for lead, kind in made]
        + [jax.ShapeDtypeStruct((rows, cols), jnp.int32)],
        compiler_params=pltpu.CompilerParams(vmem_limit_bytes=63 << 20),
        cost_estimate=pl.CostEstimate(flops=4_000_000_000, bytes_accessed=6_000_000, transcendentals=0),
    )(index, weight, blend)


def finish_kernel(
    freq, table, lists_e, lists_w, spare_e, spare_w, counts, gain, partial, motion, residual, modes, moved, even,
):
    slots, width2 = table.shape
    width = width2 // 2
    cases = width // COMP
    owners = slots // SEG

    @pl.when((pl.program_id(0) == 0) & (pl.program_id(1) == 0))
    def _():
        step = min(slots, 512)
        for b in range(slots // step):
            turned = table[b * step : b * step + step, :].astype(F32).T.astype(BF16)
            modes[:, b * step : b * step + step] = turned
            modes[0:width, slots + b * step : slots + b * step + step] = turned[0:width]
            modes[width:, slots + b * step : slots + b * step + step] = jnp.zeros((width, step), BF16)

    slot_rows = lax.broadcasted_iota(jnp.int32, (SUB, LANES), 0)
    places = [slot_rows + q * SUB for q in range(SEG // SUB)]

    def spread(ref, i, row):
        return jnp.broadcast_to(ref[i, pl.ds(row, 1), :], (SUB, LANES))

    def put(into, s, part, pairs):
        got = []
        for ids in places:
            value = 0.0
            for e, w in pairs:
                value = jnp.where(ids == e, w, value)
            got.append(value)
        high, low = halves(jnp.concatenate(got, axis=0))
        at = pl.multiple_of(s * SEG, SEG)
        into[pl.ds(at, SEG), part * LANES : part * LANES + LANES] = high
        into[pl.ds(at + slots, SEG), part * LANES : part * LANES + LANES] = low

    def product(source):
        got = jnp.dot(modes[...], source[...], preferred_element_type=F32)
        return got[0:width] + got[width:]

    def place(sums, pair, add=False):
        for part in range(2):
            for c in range(width // SUB):
                at = pl.ds(c * SUB * SUB + pair * 2 + part, SUB, stride=SUB)
                value = sums[c * SUB : c * SUB + SUB, part * LANES : part * LANES + LANES]
                moved[at, :] = moved[at, :] + value if add else value

    chunk = min(slots, 256)

    def tile(pair, first, extra):
        highs, lows = [], []
        for q in range(chunk // SEG):
            s = first + q
            sides = []
            for part in range(2):
                row = pair * 2 + part
                pairs = [(spread(lists_e, s + r * owners, row), spread(lists_w, s + r * owners, row)) for r in range(RANKS)]
                pairs += [(e - s * SEG, w) for e, w in extra[part]]
                got = []
                for ids in places:
                    value = 0.0
                    for e, w in pairs:
                        value = jnp.where(ids == e, w, value)
                    got.append(value)
                sides.append(halves(jnp.concatenate(got, axis=0)))
            highs.append(jnp.concatenate([sides[0][0], sides[1][0]], axis=1))
            lows.append(jnp.concatenate([sides[0][1], sides[1][1]], axis=1))
        return jnp.concatenate(highs, axis=0), jnp.concatenate(lows, axis=0)

    def one_pair(pair):
        extra = [[(spread(spare_e, o, pair * 2 + part), spread(spare_w, o, pair * 2 + part)) for o in range(SPARE)] for part in range(2)]
        both = rest = None
        for c in range(slots // chunk):
            high, low = tile(pair, c * (chunk // SEG), extra)
            at = slice(c * chunk, c * chunk + chunk)
            x = jnp.dot(modes[:, at], high, preferred_element_type=F32)
            y = jnp.dot(modes[0:width, at], low, preferred_element_type=F32)
            both = x if both is None else both + x
            rest = y if rest is None else rest + y
        place(both[0:width] + both[width:] + rest, pair)

    def step_pair(pair, _):
        one_pair(pair)
        return 0

    if owners <= 32:
        for pair in range(SUB // 2):
            one_pair(pair)
    else:
        lax.fori_loop(0, SUB // 2, step_pair, 0)

    count = counts[...]
    most = jnp.max(count)

    @pl.when(most > SPARE)
    def _():
        for pair in range(SUB // 2):

            def again(o, _, pair=pair):
                for part in range(2):
                    row = pair * 2 + part
                    e, w = spread(spare_e, o, row), spread(spare_w, o, row)

                    def rebuild(s, _):
                        put(even, s, part, [(e - s * SEG, w)])
                        return 0

                    lax.fori_loop(0, owners, rebuild, 0)
                place(product(even), pair, True)
                return 0

            lax.fori_loop(SPARE, jnp.max(count[pair * 2 : pair * 2 + 2]), again, 0)

    gains = [gain[i] for i in range(2 * VARS * COMP)]

    def force(c, _):
        omega = freq[c]
        m = [moved[pl.ds(pl.multiple_of((c * COMP + x) * SUB, SUB), SUB), :] for x in range(COMP)]
        for x in range(COMP):
            motion[c * COMP + x] = m[x]
        for v in range(VARS):
            pos = gains[v * COMP] * m[0]
            vel = gains[(VARS + v) * COMP] * m[0]
            for x in range(1, COMP):
                pos = pos + gains[v * COMP + x] * m[x]
                vel = vel + gains[(VARS + v) * COMP + x] * m[x]
            at = c * PARTS * VARS + v
            residual[at] = partial[at] + pos
            residual[at + VARS] = partial[at + VARS] + omega * vel
        return 0

    lax.fori_loop(0, cases, force, 0, unroll=2)


def finish(freq, table, lists, gain, partial):
    n, rows, cols = partial.shape
    slots, width2 = table.shape
    width = width2 // 2
    cells = lambda lead: pl.BlockSpec((lead, SUB, LANES), lambda b, h: (0, h, b))
    flat = pl.BlockSpec((SUB, LANES), lambda b, h: (h, b))
    return pl.pallas_call(
        finish_kernel,
        grid=(cols // LANES, rows // SUB),
        in_specs=[
            pl.BlockSpec(memory_space=pltpu.SMEM),
            pl.BlockSpec(table.shape, lambda b, h: (0, 0)),
            *[cells(x.shape[0]) for x in lists[:4]], flat, cells(gain.shape[0]), cells(n),
        ],
        out_specs=[cells(width), cells(n)],
        out_shape=[
            jax.ShapeDtypeStruct((width, rows, cols), F32),
            jax.ShapeDtypeStruct((n, rows, cols), F32),
        ],
        scratch_shapes=[
            pltpu.VMEM((width2, 2 * slots), BF16),
            pltpu.VMEM((width * SUB, LANES), F32),
            pltpu.VMEM((2 * slots, 2 * LANES), BF16),
        ],
        compiler_params=pltpu.CompilerParams(vmem_limit_bytes=63 << 20),
    )(freq, table, *lists, gain, partial)


def ring(axis, step):
    peers = lax.axis_size(axis)
    return [(i, (i + step) % peers) for i in range(peers)]


def local(mode_shapes, send_nodes, interp_index, interp_weight, blend, motion_gain, frequency, volume, jacobian, state):
    axes = ("group", "dom")
    top, bottom, first, last = faces(state)
    above = lax.ppermute(bottom, "group", ring("group", 1))
    below = lax.ppermute(top, "group", ring("group", -1))
    table = pick_nodes(mode_shapes, send_nodes, first)
    peers = lax.axis_size(axes)
    listed, width2 = table.shape
    table, first, last = lax.optimization_barrier((table, first, last))
    left = lax.ppermute(last, "dom", ring("dom", 1))
    right = lax.ppermute(first, "dom", ring("dom", -1))
    lists = owner_lists(interp_index, interp_weight, blend, listed)
    table, *lists = lax.optimization_barrier((table, *lists))
    arrived = lax.all_to_all(
        table.reshape(peers, listed // peers, width2), axes, split_axis=0, concat_axis=0, tiled=True
    ).reshape(listed, width2)
    partial = flux(frequency, volume, jacobian, state, above, below, left, right)
    return tuple(finish(frequency, arrived, lists, motion_gain, partial))


def solution(mesh):
    both = ("group", "dom")
    cells3 = P(None, "group", "dom")
    cells2 = P("group", "dom")
    placed = (P(None, both), P(both, None), cells3, cells3, cells2, cells3, P(), cells2, cells3, cells3)
    return jax.shard_map(local, mesh=mesh, in_specs=placed, out_specs=(cells3, cells3), check_vma=False)
```

time: 90.4 us -> 83.7 us (0.926)
  the two profiles are of different devices: /device:TPU:24 before, /device:TPU:0 now
where the time goes in v3:
time: 83.7 us; the launch traced here: 83.1 us
  Pallas kernels  69.8 us (83%)
  starting transfers between devices  11.1 us (13%)
  local copies, waits for them, and re-layouts  1.5 us (2%)
    pallas_call x1, Pallas kernels, flux(): pl.pallas_call(functools.partial(flux_kernel, [lax.axis_size(axis) for ax...  29.6 us
    pallas_call x1, Pallas kernels, finish(): pl.pallas_call(finish_kernel, grid=(cols // LANES, rows // SUB), in_specs...  26.9 us
    pallas_call x1, Pallas kernels, owner_lists(): pl.pallas_call(lists_kernel, grid=(cols // LANES,), in_specs=[cells(entri...  5.03 us
    pallas_call x1, Pallas kernels, faces(): pl.pallas_call(faces_kernel, in_specs=[pl.BlockSpec(memory_space=pl.ANY)]...  4.32 us
    pallas_call x1, Pallas kernels, pick_nodes(): pl.pallas_call(pick_kernel, in_specs=[vmem, vmem, pl.BlockSpec(memory_spa...  3.94 us
    all_to_all x1, starting transfers between devices, local(): lax.all_to_all(table.reshape(peers, listed // peers, width2), axes, split...  3.56 us
    ppermute x1, starting transfers between devices, local(): right = lax.ppermute(first, 'dom', ring('dom', -1))  3.54 us
    ppermute x1, starting transfers between devices, local(): above = lax.ppermute(bottom, 'group', ring('group', 1))  2.99 us
  transfers between devices with their start and end apart: 5, of which 0 were waited for; matrix products, arithmetic and copies ran while one was open for 0% of the time, Pallas kernels for 46%

profile of v3, /device:TPU:0, one launch (start us, length us, event | category | flops | bytes accessed | tf_op | source)
XLA Modules:
  0.0 83.1 jit_solution(15929745149427200448)
XLA Ops:
  0.6 4.3 %shard_map.113 = (bf16[320,512]{1,0:T(8,128)(2,1)}, bf16[320,512]{1,0:T(8,128)(2,1)}, f32[8,1,640]{2,1,0:T(1,128)}, f32[8,1,640]{2,1,0:T(1,128)}) custom-call(bf16[320,16,512]{2,1,0:T(8,128)(2,1)} %state.1), custom_call_target="tpu_custom_call" | custom-call | tf_op jit(solution)/shard_map/pallas_call | solution.py:73
  5.0 3.0 %collective-permute-start = (bf16[320,512]{1,0:T(8,128)(2,1)}, bf16[320,512]{1,0:T(8,128)(2,1)S(1)}, u32[]{:S(2)}, u32[]{:S(2)}) collective-permute-start(bf16[320,512]{1,0:T(8,128)(2,1)} %get-tuple-element.34), channel_id=1, source_target_pairs={{0,8},{8,16},{16,24},{24,0},{1,9},{9,17},{17,25},{25,1},{2,10},{10... | collective-permute-start | bytes 983048 | tf_op jit(solution)/shard_map/ppermute | solution.py:509
  7.9 1.0 %collective-permute-start.1 = (bf16[320,512]{1,0:T(8,128)(2,1)}, bf16[320,512]{1,0:T(8,128)(2,1)}, u32[]{:S(2)}, u32[]{:S(2)}) collective-permute-start(bf16[320,512]{1,0:T(8,128)(2,1)} %get-tuple-element.35), channel_id=1, source_target_pairs={{0,24},{8,0},{16,8},{24,16},{1,25},{9,1},{17,9},{25,17},{2,26},{10... | collective-permute-start | bytes 983048 | tf_op jit(solution)/shard_map/ppermute | solution.py:510
  9.0 3.9 %shard_map.114 = bf16[1024,192]{1,0:T(8,128)(2,1)} custom-call(f32[96,2048]{1,0:T(8,128)} %modes.1, s32[1,1024]{1,0:T(1,128)} %nodes.1, f32[8,1,640]{2,1,0:T(1,128)} %get-tuple-element.37.after), custom_call_target="tpu_custom_call" | custom-call | tf_op jit(solution)/shard_map/pallas_call | solution.py:120
  12.9 0.0 collective-permute-start.2
  12.9 3.5 %collective-permute-start.3 = (f32[8,1,640]{2,1,0:T(1,128)}, f32[8,1,640]{2,1,0:T(1,128)S(1)}, u32[]{:S(2)}, u32[]{:S(2)}) collective-permute-start(f32[8,1,640]{2,1,0:T(1,128)} %get-tuple-element.37.after), channel_id=1, source_target_pairs={{0,7},{1,0},{2,1},{3,2},{4,3},{5,4},{6,5},{7,6},{8,15},{9,8},{10,9... | collective-permute-start | bytes 61448 | tf_op jit(solution)/shard_map/ppermute | solution.py:516
  16.5 5.0 %shard_map.115 = (s32[64,16,512]{2,1,0:T(8,128)}, f32[64,16,512]{2,1,0:T(8,128)}, s32[6,16,512]{2,1,0:T(8,128)}, f32[6,16,512]{2,1,0:T(8,128)}, s32[16,512]{1,0:T(8,128)}) custom-call(s32[8,16,512]{2,1,0:T(8,128)} %index.1, f32[8,16,512]{2,1,0:T(8,128)} %weight.1, f32[16,512]{1,0:T(8,128)} %blend.1), custom_call_target="tpu_custom_call" | custom-call | flops 4000000000 | bytes 6000000 | tf_op jit(solution)/shard_map/pallas_call | solution.py:328
  21.5 3.6 %all-to-all-start = ((bf16[32,32,192]{2,1,0:T(8,128)(2,1)}), bf16[32,32,192]{2,1,0:T(8,128)(2,1)S(1)}, u32[]{:S(2)}, u32[]{:S(2)}) async-start(bf16[32,32,192]{2,1,0:T(8,128)(2,1)} %bitcast.3), calls=%async_computation | async-start | bytes 1048576 | tf_op jit(solution)/shard_map/all_to_all | solution.py:519
  25.1 0.0 collective-permute-done.2.left
  25.1 0.0 copy-start.2
  25.1 0.0 collective-permute-done.3.right
  25.1 0.0 copy-start.3
  25.1 0.0 collective-permute-done.above
  25.1 0.0 copy-start.1
  25.1 0.0 collective-permute-done.1.below
  25.1 0.5 copy-done.2
  25.7 0.0 copy-done.3
  25.7 0.2 copy-done.1
  25.8 29.6 %shard_map.116.partial = f32[320,16,512]{2,1,0:T(8,128)} custom-call(f32[32]{0:T(128)} %freq.3, f32[16,512]{1,0:T(8,128)} %volume.1, f32[125,16,512]{2,1,0:T(8,128)} %jac.1, bf16[320,16,512]{2,1,0:T(8,128)(2,1)} %state.1, bf16[320,512]{1,0:T(8,128)(2,1)} %copy-done.1, bf16[320,512]{1,0:T(8,128)(2,1)} %collective-permute-done.1.below, ...), custom_call_target="tpu_custom_call" | custom-call | flops 40000000000 | bytes 60000000 | tf_op jit(solution)/shard_map/pallas_call | solution.py:233
  55.5 0.0 all-to-all-done
  55.5 0.0 copy-start
  55.5 0.8 copy-done
  56.3 26.9 %shard_map.117 = (f32[96,16,512]{2,1,0:T(8,128)}, f32[320,16,512]{2,1,0:T(8,128)}) custom-call(f32[32]{0:T(128)} %freq.3, bf16[1024,192]{1,0:T(8,128)(2,1)} %bitcast.2, s32[64,16,512]{2,1,0:T(8,128)} %get-tuple-element.29.lists_e, f32[64,16,512]{2,1,0:T(8,128)} %get-tuple-element.30.lists_w, s32[6,16,512]{2,1,0:T(8,128)} %get-tuple-element.31.spare_e, ...), custom_call_target="tpu_custom_call" | custom-call | tf_op jit(solution)/shard_map/pallas_call | solution.py:479
Async XLA Ops:
  5.0 20.1 %collective-permute-start = (bf16[320,512]{1,0:T(8,128)(2,1)}, bf16[320,512]{1,0:T(8,128)(2,1)S(1)}, u32[]{:S(2)}, u32[]{:S(2)}) collective-permute-start(bf16[320,512]{1,0:T(8,128)(2,1)} %get-tuple-element.34), channel_id=1, source_target_pairs={{0,8},{8,16},{16,24},{24,0},{1,9},{9,17},{17,25},{25,1},{2,10},{10... | collective-permute-start | bytes 983048 | tf_op jit(solution)/shard_map/ppermute | solution.py:509
  7.9 17.2 %collective-permute-start.1 = (bf16[320,512]{1,0:T(8,128)(2,1)}, bf16[320,512]{1,0:T(8,128)(2,1)}, u32[]{:S(2)}, u32[]{:S(2)}) collective-permute-start(bf16[320,512]{1,0:T(8,128)(2,1)} %get-tuple-element.35), channel_id=1, source_target_pairs={{0,24},{8,0},{16,8},{24,16},{1,25},{9,1},{17,9},{25,17},{2,26},{10... | collective-permute-start | bytes 983048 | tf_op jit(solution)/shard_map/ppermute | solution.py:510
  12.9 12.2 %collective-permute-start.2 = (f32[8,1,640]{2,1,0:T(1,128)}, f32[8,1,640]{2,1,0:T(1,128)S(1)}, u32[]{:S(2)}, u32[]{:S(2)}) collective-permute-start(f32[8,1,640]{2,1,0:T(1,128)} %get-tuple-element.36), channel_id=1, source_target_pairs={{0,1},{1,2},{2,3},{3,4},{4,5},{5,6},{6,7},{7,0},{8,9},{9,10},{10,1... | collective-permute-start | bytes 61448 | tf_op jit(solution)/shard_map/ppermute | solution.py:515
  12.9 12.2 %collective-permute-start.3 = (f32[8,1,640]{2,1,0:T(1,128)}, f32[8,1,640]{2,1,0:T(1,128)S(1)}, u32[]{:S(2)}, u32[]{:S(2)}) collective-permute-start(f32[8,1,640]{2,1,0:T(1,128)} %get-tuple-element.37.after), channel_id=1, source_target_pairs={{0,7},{1,0},{2,1},{3,2},{4,3},{5,4},{6,5},{7,6},{8,15},{9,8},{10,9... | collective-permute-start | bytes 61448 | tf_op jit(solution)/shard_map/ppermute | solution.py:516
  21.5 34.0 %all-to-all-start = ((bf16[32,32,192]{2,1,0:T(8,128)(2,1)}), bf16[32,32,192]{2,1,0:T(8,128)(2,1)S(1)}, u32[]{:S(2)}, u32[]{:S(2)}) async-start(bf16[32,32,192]{2,1,0:T(8,128)(2,1)} %bitcast.3), calls=%async_computation | async-start | bytes 1048576 | tf_op jit(solution)/shard_map/all_to_all | solution.py:519
  25.1 0.6 copy-start.2
  25.1 0.6 copy-start.3
  25.1 0.7 copy-start.1
  55.5 0.8 copy-start

commit v4 on v3

--- a/solution.py
+++ b/solution.py
@@ -85,7 +85,7 @@
             pltpu.VMEM((cols // LANES, 16 * rows, LANES), F32),
             pltpu.SemaphoreType.DMA((steps,)),
         ],
-        compiler_params=pltpu.CompilerParams(vmem_limit_bytes=63 << 20),
+        compiler_params=pltpu.CompilerParams(vmem_limit_bytes=(64 << 20) - (64 << 10)),
     )(state)
 
 
@@ -110,7 +110,7 @@
         table[at, :] = total.T.astype(BF16)
         return 0
 
-    lax.fori_loop(0, listed // step, pick, 0)
+    lax.fori_loop(0, listed // step, pick, 0, unroll=4)
 
 
 def pick_nodes(modes, nodes, after):
@@ -123,7 +123,7 @@
         out_specs=vmem,
         out_shape=jax.ShapeDtypeStruct((listed, 2 * width), BF16),
         scratch_shapes=[pltpu.VMEM((2 * width, owned), BF16)],
-        compiler_params=pltpu.CompilerParams(vmem_limit_bytes=63 << 20),
+        compiler_params=pltpu.CompilerParams(vmem_limit_bytes=(64 << 20) - (64 << 10)),
     )(modes, nodes, after)
 
 
@@ -217,7 +217,7 @@
                         acc[f][v] = term if acc[f][v] is None else acc[f][v] + term
             for f in range(FIELDS):
                 for v in range(VARS):
-                    out[f * VARS + v, at, b * LANES : b * LANES + LANES] = acc[f][v]
+                    out[b, h, f * VARS + v] = acc[f][v]
             return 0
 
         lax.fori_loop(0, high, body, 0)
@@ -241,8 +241,8 @@
             pl.BlockSpec((n, cols), whole), pl.BlockSpec((n, cols), whole),
             ends, ends,
         ],
-        out_specs=pl.BlockSpec((planes, rows, cols), lambda g: (g, 0, 0)),
-        out_shape=jax.ShapeDtypeStruct((n, rows, cols), F32),
+        out_specs=pl.BlockSpec((blocks, rows // SUB, planes, SUB, LANES), lambda g: (0, 0, g, 0, 0)),
+        out_shape=jax.ShapeDtypeStruct((blocks, rows // SUB, n, SUB, LANES), F32),
         scratch_shapes=[
             pltpu.VMEM((blocks, jac.shape[0], rows, LANES), F32),
             pltpu.VMEM((blocks, planes * (rows + 2 * SUB), LANES), F32),
@@ -250,7 +250,7 @@
             pltpu.VMEM((2, n, cols), F32),
             pltpu.SemaphoreType.DMA((blocks,)),
         ],
-        compiler_params=pltpu.CompilerParams(vmem_limit_bytes=63 << 20),
+        compiler_params=pltpu.CompilerParams(vmem_limit_bytes=(64 << 20) - (64 << 10)),
         cost_estimate=pl.CostEstimate(flops=40_000_000_000, bytes_accessed=60_000_000, transcendentals=0),
     )(freq, volume, jac, state, above, below, left, right)
 
@@ -263,7 +263,11 @@
 
 def lists_kernel(index, weight, blend, lists_e, lists_w, spare_e, spare_w, counts):
     entries = index.shape[0]
-    owners = lists_e.shape[0] // RANKS
+    owners = lists_e.shape[2] // RANKS
+
+    def tile(ref, i, value):
+        for h in range(ref.shape[1]):
+            ref[0, h, i] = value[h * SUB : h * SUB + SUB]
 
     raw = [jnp.where(index[k] >= 0, weight[k], 0.0) for k in range(entries)]
     total = raw[0]
@@ -297,8 +301,8 @@
             hit = spare[k] == o
             e = jnp.where(hit, key[k], e)
             w = jnp.where(hit, share[k], w)
-        spare_e[o] = e
-        spare_w[o] = w
+        tile(spare_e, o, e)
+        tile(spare_w, o, w)
 
     local = [e & (SEG - 1) for e in key]
 
@@ -309,30 +313,31 @@
             hit = listed[k] == i
             e = jnp.where(hit, local[k], e)
             w = jnp.where(hit, share[k], w)
-        lists_e[i] = e
-        lists_w[i] = w
+        tile(lists_e, i, e)
+        tile(lists_w, i, w)
         return 0
 
     lax.fori_loop(0, owners * RANKS, fill, 0, unroll=4)
-    counts[...] = count
+    tile(counts, 0, count)
 
 
 def owner_lists(index, weight, blend, slots):
     entries, rows, cols = index.shape
     owners = slots // SEG
+    high = rows // SUB
     cells = lambda lead: pl.BlockSpec((lead, rows, LANES), lambda b: (0, 0, b))
     flat = pl.BlockSpec((rows, LANES), lambda b: (0, b))
     made = [
         (owners * RANKS, jnp.int32), (owners * RANKS, F32), (entries - RANKS, jnp.int32), (entries - RANKS, F32),
+        (1, jnp.int32),
     ]
     return pl.pallas_call(
         lists_kernel,
         grid=(cols // LANES,),
         in_specs=[cells(entries), cells(entries), flat],
-        out_specs=[cells(lead) for lead, _ in made] + [flat],
-        out_shape=[jax.ShapeDtypeStruct((lead, rows, cols), kind) for lead, kind in made]
-        + [jax.ShapeDtypeStruct((rows, cols), jnp.int32)],
-        compiler_params=pltpu.CompilerParams(vmem_limit_bytes=63 << 20),
+        out_specs=[pl.BlockSpec((1, high, lead, SUB, LANES), lambda b: (b, 0, 0, 0, 0)) for lead, _ in made],
+        out_shape=[jax.ShapeDtypeStruct((cols // LANES, high, lead, SUB, LANES), kind) for lead, kind in made],
+        compiler_params=pltpu.CompilerParams(vmem_limit_bytes=(64 << 20) - (64 << 10)),
         cost_estimate=pl.CostEstimate(flops=4_000_000_000, bytes_accessed=6_000_000, transcendentals=0),
     )(index, weight, blend)
 
@@ -427,7 +432,7 @@
     else:
         lax.fori_loop(0, SUB // 2, step_pair, 0)
 
-    count = counts[...]
+    count = counts[0]
     most = jnp.max(count)
 
     @pl.when(most > SPARE)
@@ -467,22 +472,23 @@
             residual[at + VARS] = partial[at + VARS] + omega * vel
         return 0
 
-    lax.fori_loop(0, cases, force, 0, unroll=2)
+    lax.fori_loop(0, cases, force, 0, unroll=4)
 
 
 def finish(freq, table, lists, gain, partial):
-    n, rows, cols = partial.shape
+    blocks, high, n, _, _ = partial.shape
+    rows, cols = high * SUB, blocks * LANES
     slots, width2 = table.shape
     width = width2 // 2
     cells = lambda lead: pl.BlockSpec((lead, SUB, LANES), lambda b, h: (0, h, b))
-    flat = pl.BlockSpec((SUB, LANES), lambda b, h: (h, b))
+    tiles = lambda lead: pl.BlockSpec((None, None, lead, SUB, LANES), lambda b, h: (b, h, 0, 0, 0))
     return pl.pallas_call(
         finish_kernel,
         grid=(cols // LANES, rows // SUB),
         in_specs=[
             pl.BlockSpec(memory_space=pltpu.SMEM),
             pl.BlockSpec(table.shape, lambda b, h: (0, 0)),
-            *[cells(x.shape[0]) for x in lists[:4]], flat, cells(gain.shape[0]), cells(n),
+            *[tiles(x.shape[2]) for x in lists], cells(gain.shape[0]), tiles(n),
         ],
         out_specs=[cells(width), cells(n)],
         out_shape=[
@@ -494,7 +500,7 @@
             pltpu.VMEM((width * SUB, LANES), F32),
             pltpu.VMEM((2 * slots, 2 * LANES), BF16),
         ],
-        compiler_params=pltpu.CompilerParams(vmem_limit_bytes=63 << 20),
+        compiler_params=pltpu.CompilerParams(vmem_limit_bytes=(64 << 20) - (64 << 10)),
     )(freq, table, *lists, gain, partial)
 
 

time: 83.7 us -> 81.1 us (0.969)
  local copies, waits for them, and re-layouts: 1.5 us -> 0 us
  Pallas kernels: 69.8 us -> 68.7 us
    unnamed x8 -> x0, local copies, waits for them, and re-layouts: 1.5 us -> none
  transfers between devices with their start and end apart: 5 -> 5, of which waited for: 0 -> 0; matrix products, arithmetic and copies ran while one was open for 0% -> 0% of each run, Pallas kernels for 46% -> 47%
where the time goes in v4:
time: 81.1 us; the launch traced here: 80.6 us
  Pallas kernels  68.7 us (85%)
  starting transfers between devices  11.2 us (14%)
    pallas_call x1, Pallas kernels, flux(): pl.pallas_call(functools.partial(flux_kernel, [lax.axis_size(axis) for ax...  29.7 us
    pallas_call x1, Pallas kernels, finish(): pl.pallas_call(finish_kernel, grid=(cols // LANES, rows // SUB), in_specs...  26.5 us
    pallas_call x1, Pallas kernels, owner_lists(): pl.pallas_call(lists_kernel, grid=(cols // LANES,), in_specs=[cells(entri...  4.97 us
    pallas_call x1, Pallas kernels, faces(): pl.pallas_call(faces_kernel, in_specs=[pl.BlockSpec(memory_space=pl.ANY)]...  4.32 us
    all_to_all x1, starting transfers between devices, local(): lax.all_to_all(table.reshape(peers, listed // peers, width2), axes, split...  3.69 us
    ppermute x1, starting transfers between devices, local(): right = lax.ppermute(first, 'dom', ring('dom', -1))  3.54 us
    pallas_call x1, Pallas kernels, pick_nodes(): pl.pallas_call(pick_kernel, in_specs=[vmem, vmem, pl.BlockSpec(memory_spa...  3.2 us
    ppermute x1, starting transfers between devices, local(): above = lax.ppermute(bottom, 'group', ring('group', 1))  2.99 us
  transfers between devices with their start and end apart: 5, of which 0 were waited for; matrix products, arithmetic and copies ran while one was open for 0% of the time, Pallas kernels for 47%

profile of v4, /device:TPU:0, one launch (start us, length us, event | category | flops | bytes accessed | tf_op | source)
XLA Modules:
  0.0 80.6 jit_solution(5450282424327814991)
XLA Ops:
  0.6 4.3 %shard_map.113 = (bf16[320,512]{1,0:T(8,128)(2,1)}, bf16[320,512]{1,0:T(8,128)(2,1)}, f32[8,1,640]{2,1,0:T(1,128)}, f32[8,1,640]{2,1,0:T(1,128)}) custom-call(bf16[320,16,512]{2,1,0:T(8,128)(2,1)} %state.1), custom_call_target="tpu_custom_call" | custom-call | tf_op jit(solution)/shard_map/pallas_call | solution.py:73
  5.0 3.0 %collective-permute-start = (bf16[320,512]{1,0:T(8,128)(2,1)}, bf16[320,512]{1,0:T(8,128)(2,1)}, u32[]{:S(2)}, u32[]{:S(2)}) collective-permute-start(bf16[320,512]{1,0:T(8,128)(2,1)} %get-tuple-element.34), channel_id=1, source_target_pairs={{0,8},{8,16},{16,24},{24,0},{1,9},{9,17},{17,25},{25,1},{2,10},{10... | collective-permute-start | bytes 983048 | tf_op jit(solution)/shard_map/ppermute | solution.py:515
  7.9 1.0 %collective-permute-start.1 = (bf16[320,512]{1,0:T(8,128)(2,1)}, bf16[320,512]{1,0:T(8,128)(2,1)}, u32[]{:S(2)}, u32[]{:S(2)}) collective-permute-start(bf16[320,512]{1,0:T(8,128)(2,1)} %get-tuple-element.35), channel_id=1, source_target_pairs={{0,24},{8,0},{16,8},{24,16},{1,25},{9,1},{17,9},{25,17},{2,26},{10... | collective-permute-start | bytes 983048 | tf_op jit(solution)/shard_map/ppermute | solution.py:516
  9.0 3.2 %shard_map.114 = bf16[1024,192]{1,0:T(8,128)(2,1)} custom-call(f32[96,2048]{1,0:T(8,128)} %modes.1, s32[1,1024]{1,0:T(1,128)} %nodes.1, f32[8,1,640]{2,1,0:T(1,128)} %get-tuple-element.37.after), custom_call_target="tpu_custom_call" | custom-call | tf_op jit(solution)/shard_map/pallas_call | solution.py:120
  12.2 0.0 collective-permute-start.2
  12.2 3.5 %collective-permute-start.3 = (f32[8,1,640]{2,1,0:T(1,128)}, f32[8,1,640]{2,1,0:T(1,128)}, u32[]{:S(2)}, u32[]{:S(2)}) collective-permute-start(f32[8,1,640]{2,1,0:T(1,128)} %get-tuple-element.37.after), channel_id=1, source_target_pairs={{0,7},{1,0},{2,1},{3,2},{4,3},{5,4},{6,5},{7,6},{8,15},{9,8},{10,9... | collective-permute-start | bytes 61448 | tf_op jit(solution)/shard_map/ppermute | solution.py:522
  15.7 5.0 %shard_map.115 = (s32[4,2,64,8,128]{4,3,2,1,0:T(8,128)}, f32[4,2,64,8,128]{4,3,2,1,0:T(8,128)}, s32[4,2,6,8,128]{4,3,2,1,0:T(8,128)}, f32[4,2,6,8,128]{4,3,2,1,0:T(8,128)}, s32[4,2,1,8,128]{4,3,2,1,0:T(8,128)}) custom-call(s32[8,16,512]{2,1,0:T(8,128)} %index.1, f32[8,16,512]{2,1,0:T(8,128)} %weight.1, f32[16,512]{1,0:T(8,128)} %blend.1), custom_call_target="tpu_custom_call" | custom-call | flops 4000000000 | bytes 6000000 | tf_op jit(solution)/shard_map/pallas_call | solution.py:334
  20.7 3.7 %all-to-all-start = ((bf16[32,32,192]{2,1,0:T(8,128)(2,1)}), bf16[32,32,192]{2,1,0:T(8,128)(2,1)}, u32[]{:S(2)}, u32[]{:S(2)}) async-start(bf16[32,32,192]{2,1,0:T(8,128)(2,1)} %bitcast.2), calls=%async_computation | async-start | bytes 1048576 | tf_op jit(solution)/shard_map/all_to_all | solution.py:525
  24.4 0.0 collective-permute-done.2.left
  24.4 0.0 collective-permute-done.3.right
  24.4 0.0 collective-permute-done.above
  24.4 0.0 collective-permute-done.1.below
  24.4 29.7 %shard_map.116.partial = f32[4,2,320,8,128]{4,3,2,1,0:T(8,128)} custom-call(f32[32]{0:T(128)} %freq.3, f32[16,512]{1,0:T(8,128)} %volume.1, f32[125,16,512]{2,1,0:T(8,128)} %jac.1, bf16[320,16,512]{2,1,0:T(8,128)(2,1)} %state.1, bf16[320,512]{1,0:T(8,128)(2,1)} %collective-permute-done.above, bf16[320,512]{1,0:T(8,128)(2,1)} %collective-permute-done.1.below, ...), custom_call_target="tpu_custom_call" | custom-call | flops 40000000000 | bytes 60000000 | tf_op jit(solution)/shard_map/pallas_call | solution.py:233
  54.1 0.0 all-to-all-done
  54.1 26.5 %shard_map.117 = (f32[96,16,512]{2,1,0:T(8,128)}, f32[320,16,512]{2,1,0:T(8,128)}) custom-call(f32[32]{0:T(128)} %freq.3, bf16[1024,192]{1,0:T(8,128)(2,1)} %bitcast.1.table, s32[4,2,64,8,128]{4,3,2,1,0:T(8,128)} %get-tuple-element.29.lists_e, f32[4,2,64,8,128]{4,3,2,1,0:T(8,128)} %get-tuple-element.30.lists_w, ...), custom_call_target="tpu_custom_call" | custom-call | tf_op jit(solution)/shard_map/pallas_call | solution.py:485
Async XLA Ops:
  5.0 19.5 %collective-permute-start = (bf16[320,512]{1,0:T(8,128)(2,1)}, bf16[320,512]{1,0:T(8,128)(2,1)}, u32[]{:S(2)}, u32[]{:S(2)}) collective-permute-start(bf16[320,512]{1,0:T(8,128)(2,1)} %get-tuple-element.34), channel_id=1, source_target_pairs={{0,8},{8,16},{16,24},{24,0},{1,9},{9,17},{17,25},{25,1},{2,10},{10... | collective-permute-start | bytes 983048 | tf_op jit(solution)/shard_map/ppermute | solution.py:515
  7.9 16.5 %collective-permute-start.1 = (bf16[320,512]{1,0:T(8,128)(2,1)}, bf16[320,512]{1,0:T(8,128)(2,1)}, u32[]{:S(2)}, u32[]{:S(2)}) collective-permute-start(bf16[320,512]{1,0:T(8,128)(2,1)} %get-tuple-element.35), channel_id=1, source_target_pairs={{0,24},{8,0},{16,8},{24,16},{1,25},{9,1},{17,9},{25,17},{2,26},{10... | collective-permute-start | bytes 983048 | tf_op jit(solution)/shard_map/ppermute | solution.py:516
  12.2 12.2 %collective-permute-start.2 = (f32[8,1,640]{2,1,0:T(1,128)}, f32[8,1,640]{2,1,0:T(1,128)}, u32[]{:S(2)}, u32[]{:S(2)}) collective-permute-start(f32[8,1,640]{2,1,0:T(1,128)} %get-tuple-element.36), channel_id=1, source_target_pairs={{0,1},{1,2},{2,3},{3,4},{4,5},{5,6},{6,7},{7,0},{8,9},{9,10},{10,1... | collective-permute-start | bytes 61448 | tf_op jit(solution)/shard_map/ppermute | solution.py:521
  12.2 12.2 %collective-permute-start.3 = (f32[8,1,640]{2,1,0:T(1,128)}, f32[8,1,640]{2,1,0:T(1,128)}, u32[]{:S(2)}, u32[]{:S(2)}) collective-permute-start(f32[8,1,640]{2,1,0:T(1,128)} %get-tuple-element.37.after), channel_id=1, source_target_pairs={{0,7},{1,0},{2,1},{3,2},{4,3},{5,4},{6,5},{7,6},{8,15},{9,8},{10,9... | collective-permute-start | bytes 61448 | tf_op jit(solution)/shard_map/ppermute | solution.py:522
  20.7 33.4 %all-to-all-start = ((bf16[32,32,192]{2,1,0:T(8,128)(2,1)}), bf16[32,32,192]{2,1,0:T(8,128)(2,1)}, u32[]{:S(2)}, u32[]{:S(2)}) async-start(bf16[32,32,192]{2,1,0:T(8,128)(2,1)} %bitcast.2), calls=%async_computation | async-start | bytes 1048576 | tf_op jit(solution)/shard_map/all_to_all | solution.py:525

commit v5 on v4

--- a/solution.py
+++ b/solution.py
@@ -12,7 +12,7 @@
 LANES = 128
 SUB = 8
 FIELDS = 8
-ORDER = (0, 3, 1, 4, 2)
+ORDER = (0, 1, 2, 3, 4)
 F32 = jnp.float32
 BF16 = jnp.bfloat16
 
@@ -178,6 +178,7 @@
 
             vol = volume[at, b * LANES : b * LANES + LANES]
             rates = [vol * freq[step * (FIELDS // PARTS) + c] for c in range(FIELDS // PARTS)]
+            backs = [-rate for rate in rates]
             acc = [[None] * VARS for _ in range(FIELDS)]
 
             def operand(u, d):
@@ -208,7 +209,7 @@
                 if d == 0:
                     for c in range(FIELDS // PARTS):
                         re, im = 2 * c, 2 * c + 1
-                        for f, term in ((re, -(rates[c] * q[im])), (im, rates[c] * q[re])):
+                        for f, term in ((re, backs[c] * q[im]), (im, rates[c] * q[re])):
                             acc[f][u] = term if acc[f][u] is None else acc[f][u] + term
                 for v in range(VARS):
                     j = coef[b, d * VARS * VARS + v * VARS + u, at, :]
@@ -472,7 +473,7 @@
             residual[at + VARS] = partial[at + VARS] + omega * vel
         return 0
 
-    lax.fori_loop(0, cases, force, 0, unroll=4)
+    lax.fori_loop(0, cases, force, 0, unroll=8)
 
 
 def finish(freq, table, lists, gain, partial):

time: 81.1 us -> 81 us (level)
  no operation moved by 1% of the time
where the time goes in v5:
time: 81 us; the launch traced here: 80.1 us
  Pallas kernels  68.2 us (84%)
  starting transfers between devices  11.2 us (14%)
    pallas_call x1, Pallas kernels, flux(): pl.pallas_call(functools.partial(flux_kernel, [lax.axis_size(axis) for ax...  29.4 us
    pallas_call x1, Pallas kernels, finish(): pl.pallas_call(finish_kernel, grid=(cols // LANES, rows // SUB), in_specs...  26.3 us
    pallas_call x1, Pallas kernels, owner_lists(): pl.pallas_call(lists_kernel, grid=(cols // LANES,), in_specs=[cells(entri...  4.97 us
    pallas_call x1, Pallas kernels, faces(): pl.pallas_call(faces_kernel, in_specs=[pl.BlockSpec(memory_space=pl.ANY)]...  4.32 us
    all_to_all x1, starting transfers between devices, local(): lax.all_to_all(table.reshape(peers, listed // peers, width2), axes, split...  3.69 us
    ppermute x1, starting transfers between devices, local(): right = lax.ppermute(first, 'dom', ring('dom', -1))  3.54 us
    pallas_call x1, Pallas kernels, pick_nodes(): pl.pallas_call(pick_kernel, in_specs=[vmem, vmem, pl.BlockSpec(memory_spa...  3.2 us
    ppermute x1, starting transfers between devices, local(): above = lax.ppermute(bottom, 'group', ring('group', 1))  2.99 us
  transfers between devices with their start and end apart: 5, of which 0 were waited for; matrix products, arithmetic and copies ran while one was open for 0% of the time, Pallas kernels for 47%

profile of v5, /device:TPU:0, one launch (start us, length us, event | category | flops | bytes accessed | tf_op | source)
XLA Modules:
  0.0 80.1 jit_solution(6017432046770708991)
XLA Ops:
  0.6 4.3 %shard_map.113 = (bf16[320,512]{1,0:T(8,128)(2,1)}, bf16[320,512]{1,0:T(8,128)(2,1)}, f32[8,1,640]{2,1,0:T(1,128)}, f32[8,1,640]{2,1,0:T(1,128)}) custom-call(bf16[320,16,512]{2,1,0:T(8,128)(2,1)} %state.1), custom_call_target="tpu_custom_call" | custom-call | tf_op jit(solution)/shard_map/pallas_call | solution.py:73
  5.0 3.0 %collective-permute-start = (bf16[320,512]{1,0:T(8,128)(2,1)}, bf16[320,512]{1,0:T(8,128)(2,1)}, u32[]{:S(2)}, u32[]{:S(2)}) collective-permute-start(bf16[320,512]{1,0:T(8,128)(2,1)} %get-tuple-element.34), channel_id=1, source_target_pairs={{0,8},{8,16},{16,24},{24,0},{1,9},{9,17},{17,25},{25,1},{2,10},{10... | collective-permute-start | bytes 983048 | tf_op jit(solution)/shard_map/ppermute | solution.py:516
  7.9 1.0 %collective-permute-start.1 = (bf16[320,512]{1,0:T(8,128)(2,1)}, bf16[320,512]{1,0:T(8,128)(2,1)}, u32[]{:S(2)}, u32[]{:S(2)}) collective-permute-start(bf16[320,512]{1,0:T(8,128)(2,1)} %get-tuple-element.35), channel_id=1, source_target_pairs={{0,24},{8,0},{16,8},{24,16},{1,25},{9,1},{17,9},{25,17},{2,26},{10... | collective-permute-start | bytes 983048 | tf_op jit(solution)/shard_map/ppermute | solution.py:517
  9.0 3.2 %shard_map.114 = bf16[1024,192]{1,0:T(8,128)(2,1)} custom-call(f32[96,2048]{1,0:T(8,128)} %modes.1, s32[1,1024]{1,0:T(1,128)} %nodes.1, f32[8,1,640]{2,1,0:T(1,128)} %get-tuple-element.37.after), custom_call_target="tpu_custom_call" | custom-call | tf_op jit(solution)/shard_map/pallas_call | solution.py:120
  12.2 0.0 collective-permute-start.2
  12.2 3.5 %collective-permute-start.3 = (f32[8,1,640]{2,1,0:T(1,128)}, f32[8,1,640]{2,1,0:T(1,128)}, u32[]{:S(2)}, u32[]{:S(2)}) collective-permute-start(f32[8,1,640]{2,1,0:T(1,128)} %get-tuple-element.37.after), channel_id=1, source_target_pairs={{0,7},{1,0},{2,1},{3,2},{4,3},{5,4},{6,5},{7,6},{8,15},{9,8},{10,9... | collective-permute-start | bytes 61448 | tf_op jit(solution)/shard_map/ppermute | solution.py:523
  15.7 5.0 %shard_map.115 = (s32[4,2,64,8,128]{4,3,2,1,0:T(8,128)}, f32[4,2,64,8,128]{4,3,2,1,0:T(8,128)}, s32[4,2,6,8,128]{4,3,2,1,0:T(8,128)}, f32[4,2,6,8,128]{4,3,2,1,0:T(8,128)}, s32[4,2,1,8,128]{4,3,2,1,0:T(8,128)}) custom-call(s32[8,16,512]{2,1,0:T(8,128)} %index.1, f32[8,16,512]{2,1,0:T(8,128)} %weight.1, f32[16,512]{1,0:T(8,128)} %blend.1), custom_call_target="tpu_custom_call" | custom-call | flops 4000000000 | bytes 6000000 | tf_op jit(solution)/shard_map/pallas_call | solution.py:335
  20.7 3.7 %all-to-all-start = ((bf16[32,32,192]{2,1,0:T(8,128)(2,1)}), bf16[32,32,192]{2,1,0:T(8,128)(2,1)}, u32[]{:S(2)}, u32[]{:S(2)}) async-start(bf16[32,32,192]{2,1,0:T(8,128)(2,1)} %bitcast.2), calls=%async_computation | async-start | bytes 1048576 | tf_op jit(solution)/shard_map/all_to_all | solution.py:526
  24.4 0.0 collective-permute-done.2.left
  24.4 0.0 collective-permute-done.3.right
  24.4 0.0 collective-permute-done.above
  24.4 0.0 collective-permute-done.1.below
  24.4 29.4 %shard_map.116.partial = f32[4,2,320,8,128]{4,3,2,1,0:T(8,128)} custom-call(f32[32]{0:T(128)} %freq.3, f32[16,512]{1,0:T(8,128)} %volume.1, f32[125,16,512]{2,1,0:T(8,128)} %jac.1, bf16[320,16,512]{2,1,0:T(8,128)(2,1)} %state.1, bf16[320,512]{1,0:T(8,128)(2,1)} %collective-permute-done.above, bf16[320,512]{1,0:T(8,128)(2,1)} %collective-permute-done.1.below, ...), custom_call_target="tpu_custom_call" | custom-call | flops 40000000000 | bytes 60000000 | tf_op jit(solution)/shard_map/pallas_call | solution.py:234
  53.8 0.0 all-to-all-done
  53.8 26.3 %shard_map.117 = (f32[96,16,512]{2,1,0:T(8,128)}, f32[320,16,512]{2,1,0:T(8,128)}) custom-call(f32[32]{0:T(128)} %freq.3, bf16[1024,192]{1,0:T(8,128)(2,1)} %bitcast.1.table, s32[4,2,64,8,128]{4,3,2,1,0:T(8,128)} %get-tuple-element.29.lists_e, f32[4,2,64,8,128]{4,3,2,1,0:T(8,128)} %get-tuple-element.30.lists_w, ...), custom_call_target="tpu_custom_call" | custom-call | tf_op jit(solution)/shard_map/pallas_call | solution.py:486
Async XLA Ops:
  5.0 19.5 %collective-permute-start = (bf16[320,512]{1,0:T(8,128)(2,1)}, bf16[320,512]{1,0:T(8,128)(2,1)}, u32[]{:S(2)}, u32[]{:S(2)}) collective-permute-start(bf16[320,512]{1,0:T(8,128)(2,1)} %get-tuple-element.34), channel_id=1, source_target_pairs={{0,8},{8,16},{16,24},{24,0},{1,9},{9,17},{17,25},{25,1},{2,10},{10... | collective-permute-start | bytes 983048 | tf_op jit(solution)/shard_map/ppermute | solution.py:516
  7.9 16.5 %collective-permute-start.1 = (bf16[320,512]{1,0:T(8,128)(2,1)}, bf16[320,512]{1,0:T(8,128)(2,1)}, u32[]{:S(2)}, u32[]{:S(2)}) collective-permute-start(bf16[320,512]{1,0:T(8,128)(2,1)} %get-tuple-element.35), channel_id=1, source_target_pairs={{0,24},{8,0},{16,8},{24,16},{1,25},{9,1},{17,9},{25,17},{2,26},{10... | collective-permute-start | bytes 983048 | tf_op jit(solution)/shard_map/ppermute | solution.py:517
  12.2 12.2 %collective-permute-start.2 = (f32[8,1,640]{2,1,0:T(1,128)}, f32[8,1,640]{2,1,0:T(1,128)}, u32[]{:S(2)}, u32[]{:S(2)}) collective-permute-start(f32[8,1,640]{2,1,0:T(1,128)} %get-tuple-element.36), channel_id=1, source_target_pairs={{0,1},{1,2},{2,3},{3,4},{4,5},{5,6},{6,7},{7,0},{8,9},{9,10},{10,1... | collective-permute-start | bytes 61448 | tf_op jit(solution)/shard_map/ppermute | solution.py:522
  12.2 12.2 %collective-permute-start.3 = (f32[8,1,640]{2,1,0:T(1,128)}, f32[8,1,640]{2,1,0:T(1,128)}, u32[]{:S(2)}, u32[]{:S(2)}) collective-permute-start(f32[8,1,640]{2,1,0:T(1,128)} %get-tuple-element.37.after), channel_id=1, source_target_pairs={{0,7},{1,0},{2,1},{3,2},{4,3},{5,4},{6,5},{7,6},{8,15},{9,8},{10,9... | collective-permute-start | bytes 61448 | tf_op jit(solution)/shard_map/ppermute | solution.py:523
  20.7 33.1 %all-to-all-start = ((bf16[32,32,192]{2,1,0:T(8,128)(2,1)}), bf16[32,32,192]{2,1,0:T(8,128)(2,1)}, u32[]{:S(2)}, u32[]{:S(2)}) async-start(bf16[32,32,192]{2,1,0:T(8,128)(2,1)} %bitcast.2), calls=%async_computation | async-start | bytes 1048576 | tf_op jit(solution)/shard_map/all_to_all | solution.py:526
